TPU v7x, 32 devices: a whole 2x2x4 slice. The times are simulated.
32 devices in a mesh: dp: 16 (over z, y, core), tensor: 2 (over x).
Axes of the slice: x: 2, y: 2, z: 4, core: 2. Of those that a mesh axis runs over, the one named last changes fastest.
Arguments:
- tokens: int32 [32, 1024], P('dp'), may hold values from 0 to 255
- targets: int32 [32, 1024], P('dp'), may hold values from 0 to 255
- boundaries: int32 [32, 1024], P('dp'), may hold values from 0 to 1, as said below
- lengths: int32 [32], P('dp'), may hold values from 128 to 1024
- embedding: float32 [256, 512], replicated, may hold values from -6 to 6
- head: float32 [512, 256], replicated, may hold values from -0.25 to 0.25
- qkv_weight: float32 [3, 512, 3, 512], P(None, None, None, 'tensor'), may hold values from -0.25 to 0.25
- out_weight: float32 [3, 512, 512], P(None, 'tensor')
- up_weight: float32 [3, 512, 2048], P(None, None, 'tensor'), may hold values from -0.25 to 0.25
- up_bias: float32 [3, 2048], P(None, 'tensor'), may hold values from -1.8 to 1.8
- down_weight: float32 [3, 2048, 512], P(None, 'tensor')
- gains: float32 [7, 512], replicated, may hold values from 0.5 to 1.5
- boundary_weight: float32 [512], replicated, may hold values from -0.25 to 0.25
- qkv_moment: float32 [3, 512, 3, 512], P(None, None, None, 'tensor')
- out_moment: float32 [3, 512, 512], P(None, 'tensor')
- up_moment: float32 [3, 512, 2048], P(None, None, 'tensor')
- down_moment: float32 [3, 2048, 512], P(None, 'tensor')
- embedding_first: float32 [256, 512], replicated
- embedding_second: float32 [256, 512], replicated
- head_first: float32 [512, 256], replicated
- head_second: float32 [512, 256], replicated
- gains_first: float32 [7, 512], replicated
- gains_second: float32 [7, 512], replicated
- bias_first: float32 [3, 2048], P(None, 'tensor')
- bias_second: float32 [3, 2048], P(None, 'tensor')
- boundary_first: float32 [512], replicated
- boundary_second: float32 [512], replicated
Outputs:
- loss_sum: float32 [], replicated
- token_count: float32 [], replicated
- grad_norm: float32 [], replicated
- qkv_moment_new: float32 [3, 512, 3, 512], P(None, None, None, 'tensor')
- qkv_new: float32 [3, 512, 3, 512], P(None, None, None, 'tensor')
- out_moment_new: float32 [3, 512, 512], P(None, 'tensor')
- out_new: float32 [3, 512, 512], P(None, 'tensor')
- up_moment_new: float32 [3, 512, 2048], P(None, None, 'tensor')
- up_new: float32 [3, 512, 2048], P(None, None, 'tensor')
- down_moment_new: float32 [3, 2048, 512], P(None, 'tensor')
- down_new: float32 [3, 2048, 512], P(None, 'tensor')
- embedding_first_new: float32 [256, 512], replicated
- embedding_second_new: float32 [256, 512], replicated
- embedding_new: float32 [256, 512], replicated
- head_first_new: float32 [512, 256], replicated
- head_second_new: float32 [512, 256], replicated
- head_new: float32 [512, 256], replicated
- gains_first_new: float32 [7, 512], replicated
- gains_second_new: float32 [7, 512], replicated
- gains_new: float32 [7, 512], replicated
- bias_first_new: float32 [3, 2048], P(None, 'tensor')
- bias_second_new: float32 [3, 2048], P(None, 'tensor')
- bias_new: float32 [3, 2048], P(None, 'tensor')
- boundary_first_new: float32 [512], replicated
- boundary_second_new: float32 [512], replicated
- boundary_new: float32 [512], replicated
Inputs may be any that keep to these rules, and one draw needn't show every extreme that they name: `boundaries`: each sequence holds exactly 160 segments; the last byte of every sequence is a 1.
All inputs are finite; a program needn't handle non-finite values.
Results may differ from a plain program's by a relative error of at most 0.025.
Values may be sent and summed in bfloat16 or wider, within the bound.
No kernel may reach another device: no remote copies, remote signals or barrier semaphores. Data moves between devices by JAX's collectives and lax.ppermute only.
A program may use at most 448 MiB of HBM per device.

v0:
```python
import math

import jax
import jax.numpy as jnp
from jax import lax
from jax.sharding import PartitionSpec as P

HEAD_SIZE = 64
VOCAB = 256
LAYERS = 3
SHORT = 160
STEP = 10


NORM_EPSILON = 1e-06
PRIOR_RATE = 0.25
CLIP_NORM = 0.05
MOMENTUM = 0.95
MUON_DECAY = 0.01
MUON_RATE = 4.0
BETA_ONE = 0.9
BETA_TWO = 0.95
ADAM_EPSILON = 1e-08
COEF_A = 3.4445
COEF_B = -4.775
COEF_C = 2.0315


def shortened_2(value):
    return jax.tree.map(lambda a: a.astype(jnp.bfloat16) if a.dtype == jnp.float32 else a, value)


def from_root(value, axis, source):
    kept = jnp.where(lax.axis_index(axis) == source, value, 0).astype(value.dtype)
    return lax.psum(kept, axis)


def matmul_exact(left, right):
    return jnp.dot(left, right, precision=lax.Precision.HIGHEST)


def rms_norm(values, gain_row):
    return (
        values
        * lax.rsqrt(jnp.mean(values * values, axis=-1, keepdims=True) + NORM_EPSILON)
        * gain_row
    )


def block_rows(total):
    return 512 if total % 512 == 0 else total


def causal_scores(queries, key_rows, first_row):
    scores = jnp.einsum(
        "sqhd,skhd->shqk", queries, key_rows, preferred_element_type=jnp.float32
    ) * queries.shape[-1] ** (-0.5)
    row_index = first_row + jnp.arange(queries.shape[1])
    allowed = row_index[:, None] >= jnp.arange(key_rows.shape[1])[None, :]
    return jnp.where(allowed, scores, -1e30)


def attend(queries, key_rows, value_rows):
    total = queries.shape[1]
    step_rows = block_rows(total)
    outputs = []
    summaries = []
    for first_row in range(0, total, step_rows):
        scores = causal_scores(queries[:, first_row : first_row + step_rows], key_rows, first_row)
        highest = jnp.max(scores, axis=-1, keepdims=True)
        expo = jnp.exp(scores - highest)
        totals = jnp.sum(expo, axis=-1, keepdims=True)
        softened = (expo / totals).astype(jnp.bfloat16)
        outputs.append(
            jnp.einsum(
                "shqk,skhd->sqhd", softened, value_rows, preferred_element_type=jnp.float32
            ).astype(jnp.bfloat16)
        )
        summaries.append(highest[..., 0] + jnp.log(totals[..., 0]))
    return (jnp.concatenate(outputs, axis=1), jnp.concatenate(summaries, axis=2))


def attend_back(queries, key_rows, value_rows, grad_mixed, summary):
    total = queries.shape[1]
    step_rows = block_rows(total)
    scale = queries.shape[-1] ** (-0.5)
    grad_keys = jnp.zeros(key_rows.shape, jnp.float32)
    grad_values = jnp.zeros(value_rows.shape, jnp.float32)
    grad_queries = []
    for first_row in range(0, total, step_rows):
        query_block = queries[:, first_row : first_row + step_rows]
        scores = causal_scores(query_block, key_rows, first_row)
        soft = jnp.exp(scores - summary[:, :, first_row : first_row + step_rows, None])
        grad_block = grad_mixed[:, first_row : first_row + step_rows]
        grad_values = grad_values + jnp.einsum(
            "shqk,sqhd->skhd",
            soft.astype(jnp.bfloat16),
            grad_block,
            preferred_element_type=jnp.float32,
        )
        grad_soft = jnp.einsum(
            "sqhd,skhd->shqk", grad_block, value_rows, preferred_element_type=jnp.float32
        )
        centre = jnp.sum(grad_soft * soft, axis=-1, keepdims=True)
        grad_scores = (soft * (grad_soft - centre)).astype(jnp.bfloat16)
        grad_queries.append(
            scale
            * jnp.einsum(
                "shqk,skhd->sqhd", grad_scores, key_rows, preferred_element_type=jnp.float32
            )
        )
        grad_keys = grad_keys + scale * jnp.einsum(
            "shqk,sqhd->skhd", grad_scores, query_block, preferred_element_type=jnp.float32
        )
    return (jnp.concatenate(grad_queries, axis=1), grad_keys, grad_values)


def split_packed(packed, sequences):
    rows_all = packed.shape[0]
    return packed.reshape(
        sequences, rows_all // sequences, 3, packed.shape[2] // HEAD_SIZE, HEAD_SIZE
    )


def layer_forward(inputs, sequences, weights):
    gain_pair, w_qkv, w_out, w_up, b_up, w_down = weights
    rows_all = inputs.shape[0]
    normed = rms_norm(inputs, gain_pair[0]).astype(jnp.bfloat16)
    packed = jnp.einsum(
        "rd,dcf->rcf", normed, w_qkv.astype(jnp.bfloat16), preferred_element_type=jnp.float32
    ).astype(jnp.bfloat16)
    split = split_packed(packed, sequences)
    mixed, summary = attend(split[:, :, 0], split[:, :, 1], split[:, :, 2])
    partial_attn = jnp.dot(
        mixed.reshape(rows_all, -1), w_out.astype(jnp.bfloat16), preferred_element_type=jnp.float32
    )
    after = inputs + lax.psum(partial_attn.astype(jnp.bfloat16), "tensor").astype(jnp.float32)
    normed_ffn = rms_norm(after, gain_pair[1]).astype(jnp.bfloat16)
    hidden = (
        jnp.dot(normed_ffn, w_up.astype(jnp.bfloat16), preferred_element_type=jnp.float32) + b_up
    )
    activated = jax.nn.gelu(hidden).astype(jnp.bfloat16)
    partial_ffn = jnp.dot(
        activated, w_down.astype(jnp.bfloat16), preferred_element_type=jnp.float32
    )
    result = after + lax.psum(partial_ffn.astype(jnp.bfloat16), "tensor").astype(jnp.float32)
    return (result, (inputs, after, packed, mixed, summary, hidden))


def layer_backward(grad_result, saved, sequences, weights):
    gain_pair, w_qkv, w_out, w_up, b_up, w_down = weights
    inputs, after, packed, mixed, summary, hidden = saved
    rows_all = inputs.shape[0]
    grad_branch = grad_result.astype(jnp.bfloat16)
    activated, gelu_back = jax.vjp(jax.nn.gelu, hidden)
    grad_down = jnp.dot(
        activated.astype(jnp.bfloat16).T, grad_branch, preferred_element_type=jnp.float32
    )
    grad_act = jnp.dot(
        grad_branch, w_down.astype(jnp.bfloat16).T, preferred_element_type=jnp.float32
    )
    grad_hidden = gelu_back(grad_act)[0].astype(jnp.bfloat16)
    grad_bias = jnp.sum(grad_hidden.astype(jnp.float32), axis=0)
    normed_ffn, norm_back_two = jax.vjp(rms_norm, after, gain_pair[1])
    grad_up = jnp.dot(
        normed_ffn.astype(jnp.bfloat16).T, grad_hidden, preferred_element_type=jnp.float32
    )
    partial_ffn = jnp.dot(
        grad_hidden, w_up.astype(jnp.bfloat16).T, preferred_element_type=jnp.float32
    )
    grad_normed_ffn = lax.psum(partial_ffn.astype(jnp.bfloat16), "tensor").astype(jnp.float32)
    grad_after_norm, grad_gain_two = norm_back_two(grad_normed_ffn)
    grad_after = grad_result + grad_after_norm
    grad_attn = grad_after.astype(jnp.bfloat16)
    flat_mixed = mixed.reshape(rows_all, -1)
    grad_out = jnp.dot(flat_mixed.T, grad_attn, preferred_element_type=jnp.float32)
    grad_mixed = (
        jnp.dot(grad_attn, w_out.astype(jnp.bfloat16).T, preferred_element_type=jnp.float32)
        .astype(jnp.bfloat16)
        .reshape(mixed.shape)
    )
    split = split_packed(packed, sequences)
    grad_q, grad_k, grad_v = attend_back(
        split[:, :, 0], split[:, :, 1], split[:, :, 2], grad_mixed, summary
    )
    grad_packed = (
        jnp.stack([grad_q, grad_k, grad_v], axis=2).astype(jnp.bfloat16).reshape(rows_all, 3, -1)
    )
    normed, norm_back_one = jax.vjp(rms_norm, inputs, gain_pair[0])
    grad_qkv = jnp.einsum(
        "rd,rcf->dcf", normed.astype(jnp.bfloat16), grad_packed, preferred_element_type=jnp.float32
    )
    partial_attn = jnp.einsum(
        "rcf,dcf->rd", grad_packed, w_qkv.astype(jnp.bfloat16), preferred_element_type=jnp.float32
    )
    grad_normed = lax.psum(partial_attn.astype(jnp.bfloat16), "tensor").astype(jnp.float32)
    grad_inputs_norm, grad_gain_one = norm_back_one(grad_normed)
    grads = (
        jnp.stack([grad_gain_one, grad_gain_two]),
        grad_qkv,
        grad_out,
        grad_up,
        grad_bias,
        grad_down,
    )
    return (grad_after + grad_inputs_norm, grads)


def newton_schulz(matrix):
    is_tall = matrix.shape[0] > matrix.shape[1]
    current = matrix.T if is_tall else matrix
    current = current / (jnp.sqrt(jnp.sum(current * current)) + 1e-07)
    for _ in range(5):
        gram_matrix = matmul_exact(current, current.T)
        polynomial = COEF_B * gram_matrix + COEF_C * matmul_exact(gram_matrix, gram_matrix)
        current = COEF_A * current + matmul_exact(polynomial, current)
    return current.T if is_tall else current


def blank_matrix(matrix):
    return jnp.zeros_like(matrix)


def adam_update(weight, first, second, grad, rate, decay):
    first = BETA_ONE * first + (1.0 - BETA_ONE) * grad
    second = BETA_TWO * second + (1.0 - BETA_TWO) * grad * grad
    corrected = (
        first / (1.0 - BETA_ONE**STEP) / (jnp.sqrt(second / (1.0 - BETA_TWO**STEP)) + ADAM_EPSILON)
    )
    return (first, second, weight * (1.0 - rate * decay) - rate * corrected)


def body(
    tokens,
    targets,
    boundaries,
    lengths,
    embedding,
    head,
    qkv_weight,
    out_weight,
    up_weight,
    up_bias,
    down_weight,
    gains,
    boundary_weight,
    qkv_moment,
    out_moment,
    up_moment,
    down_moment,
    embedding_first,
    embedding_second,
    head_first,
    head_second,
    gains_first,
    gains_second,
    bias_first,
    bias_second,
    boundary_first,
    boundary_second,
):
    sequences, length = tokens.shape
    rows_all = sequences * length
    vocab_ids = jnp.arange(VOCAB, dtype=jnp.int32)
    token_hot = (tokens.reshape(rows_all, 1) == vocab_ids[None, :]).astype(jnp.float32)
    target_hot = (targets.reshape(rows_all, 1) == vocab_ids[None, :]).astype(jnp.float32)
    counted = (
        (jnp.arange(length, dtype=jnp.int32)[None, :] < lengths[:, None])
        .astype(jnp.float32)
        .reshape(rows_all)
    )
    segment = jnp.cumsum(boundaries, axis=1) - boundaries
    short_ids = jnp.arange(SHORT, dtype=jnp.int32)
    pool_hot = (segment[:, None, :] == short_ids[None, :, None]).astype(jnp.bfloat16)
    lift_hot = (segment[:, :, None] - 1 == short_ids[None, None, :]).astype(jnp.bfloat16)
    sizes_seg = jnp.sum(pool_hot.astype(jnp.float32), axis=2, keepdims=True)

    def layer_weights(index):
        return (
            gains[2 * index : 2 * index + 2],
            qkv_weight[index],
            out_weight[index],
            up_weight[index],
            up_bias[index],
            down_weight[index],
        )

    start_rows = matmul_exact(token_hot, embedding)
    first_out, saved_one = layer_forward(start_rows, sequences, layer_weights(0))
    bound_prob = jax.nn.sigmoid(matmul_exact(first_out, boundary_weight))
    first_low = first_out.astype(jnp.bfloat16).reshape(sequences, length, -1)
    shortened = (
        jnp.einsum("sjt,std->sjd", pool_hot, first_low, preferred_element_type=jnp.float32)
        / sizes_seg
    ).reshape(sequences * SHORT, -1)
    short_out, saved_two = layer_forward(shortened, sequences, layer_weights(1))
    short_low = short_out.astype(jnp.bfloat16).reshape(sequences, SHORT, -1)
    lifted = jnp.einsum(
        "stj,sjd->std", lift_hot, short_low, preferred_element_type=jnp.float32
    ).reshape(rows_all, -1)
    final_out, saved_three = layer_forward(first_out + lifted, sequences, layer_weights(2))
    final_norm, final_back = jax.vjp(rms_norm, final_out, gains[2 * LAYERS])
    final_low = final_norm.astype(jnp.bfloat16)
    head_low = head.astype(jnp.bfloat16)
    logits = jnp.dot(final_low, head_low, preferred_element_type=jnp.float32)
    highest = jnp.max(logits, axis=-1, keepdims=True)
    log_probs = (
        logits - highest - jnp.log(jnp.sum(jnp.exp(logits - highest), axis=-1, keepdims=True))
    )
    local_cross = -jnp.sum(counted * jnp.sum(target_hot * log_probs, axis=-1))
    bound_total, count_total, cross_total = lax.psum(
        (jnp.sum(counted * bound_prob), jnp.sum(counted), local_cross), "dp"
    )
    rest_count = count_total - bound_total
    prior_nll = -(
        lax.lgamma(count_total + 1.0)
        - lax.lgamma(bound_total + 1.0)
        - lax.lgamma(rest_count + 1.0)
        + bound_total * math.log(PRIOR_RATE)
        + rest_count * math.log(1.0 - PRIOR_RATE)
    )
    loss_sum = cross_total + prior_nll
    prior_slope = (
        lax.digamma(bound_total + 1.0)
        - lax.digamma(rest_count + 1.0)
        - math.log(PRIOR_RATE)
        + math.log(1.0 - PRIOR_RATE)
    ) / count_total
    grad_logits = ((jnp.exp(log_probs) - target_hot) * (counted / count_total)[:, None]).astype(
        jnp.bfloat16
    )
    grad_head = jnp.dot(final_low.T, grad_logits, preferred_element_type=jnp.float32)
    grad_final, grad_final_gain = final_back(
        jnp.dot(grad_logits, head_low.T, preferred_element_type=jnp.float32)
    )
    grad_merged, grads_three = layer_backward(grad_final, saved_three, sequences, layer_weights(2))
    grad_lift = grad_merged.astype(jnp.bfloat16).reshape(sequences, length, -1)
    grad_short = jnp.einsum(
        "stj,std->sjd", lift_hot, grad_lift, preferred_element_type=jnp.float32
    ).reshape(sequences * SHORT, -1)
    grad_pooled, grads_two = layer_backward(grad_short, saved_two, sequences, layer_weights(1))
    pooled_low = (grad_pooled.reshape(sequences, SHORT, -1) / sizes_seg).astype(jnp.bfloat16)
    prior_term = prior_slope * counted * bound_prob * (1.0 - bound_prob)
    grad_first = (
        grad_merged
        + jnp.einsum(
            "sjt,sjd->std", pool_hot, pooled_low, preferred_element_type=jnp.float32
        ).reshape(rows_all, -1)
        + prior_term[:, None] * boundary_weight[None, :]
    )
    grad_bound = matmul_exact(prior_term, first_out)
    grad_start, grads_one = layer_backward(grad_first, saved_one, sequences, layer_weights(0))
    grad_embed = matmul_exact(token_hot.T, grad_start)
    stacked = [
        jnp.stack([one_part, two_part, three_part])
        for one_part, two_part, three_part in zip(grads_one, grads_two, grads_three)
    ]
    summed = (
        lax.psum(stacked[0].astype(jnp.bfloat16), "dp").astype(jnp.float32),
        lax.psum(stacked[1].astype(jnp.bfloat16), "dp").astype(jnp.float32),
        lax.psum(stacked[2].astype(jnp.bfloat16), "dp").astype(jnp.float32),
        lax.psum(stacked[3].astype(jnp.bfloat16), "dp").astype(jnp.float32),
        lax.psum(stacked[4].astype(jnp.bfloat16), "dp").astype(jnp.float32),
        lax.psum(stacked[5].astype(jnp.bfloat16), "dp").astype(jnp.float32),
        lax.psum(grad_embed.astype(jnp.bfloat16), "dp").astype(jnp.float32),
        lax.psum(grad_head.astype(jnp.bfloat16), "dp").astype(jnp.float32),
        lax.psum(grad_final_gain.astype(jnp.bfloat16), "dp").astype(jnp.float32),
        lax.psum(grad_bound.astype(jnp.bfloat16), "dp").astype(jnp.float32),
    )
    stacked = list(summed[:6])
    grad_embed, grad_head, grad_final_gain, grad_bound = (
        summed[6],
        summed[7],
        summed[8],
        summed[9],
    )
    grad_gains = jnp.concatenate(
        [stacked[0].reshape(2 * LAYERS, -1), grad_final_gain[None, :]], axis=0
    )
    grad_qkv, grad_out, grad_up, grad_bias, grad_down = (
        stacked[1],
        stacked[2],
        stacked[3],
        stacked[4],
        stacked[5],
    )
    split_squares = sum(
        (jnp.sum(grad * grad) for grad in (grad_qkv, grad_out, grad_up, grad_bias, grad_down))
    )
    shared_squares = sum(
        (jnp.sum(grad * grad) for grad in (grad_embed, grad_head, grad_gains, grad_bound))
    )
    grad_norm = jnp.sqrt(lax.psum(split_squares, "tensor") + shared_squares)
    factor = jnp.minimum(1.0, CLIP_NORM / (grad_norm + 1e-06))
    kinds = (
        (qkv_weight, qkv_moment, grad_qkv * factor, 2),
        (out_weight, out_moment, grad_out * factor, 0),
        (up_weight, up_moment, grad_up * factor, 1),
        (down_weight, down_moment, grad_down * factor, 0),
    )
    dp_place = lax.axis_index("dp")
    tensor_place = lax.axis_index("tensor")
    owner_base = lax.axis_size("dp") - 4 * LAYERS
    new_moments = []
    selected = []
    for kind_index in range(4):
        weight, moment, grad, split_dim = kinds[kind_index]
        new_moment = MOMENTUM * moment + grad
        blend = grad + MOMENTUM * new_moment
        chosen = jnp.clip(dp_place - owner_base - kind_index * LAYERS, 0, LAYERS - 1)
        new_moments.append(new_moment)
        selected.append(lax.dynamic_index_in_dim(blend, chosen, 0, keepdims=False))
    gathered = (
        lax.all_gather(selected[0].astype(jnp.bfloat16), "tensor", axis=2, tiled=True).astype(
            jnp.float32
        ),
        lax.all_gather(selected[1].astype(jnp.bfloat16), "tensor", axis=0, tiled=True).astype(
            jnp.float32
        ),
        lax.all_gather(selected[2].astype(jnp.bfloat16), "tensor", axis=1, tiled=True).astype(
            jnp.float32
        ),
        lax.all_gather(selected[3].astype(jnp.bfloat16), "tensor", axis=0, tiled=True).astype(
            jnp.float32
        ),
    )
    own_shards = []
    scales = []
    for kind_index in range(4):
        split_dim = kinds[kind_index][3]
        whole = gathered[kind_index]
        flat = whole.reshape(whole.shape[0], -1)
        first_owner = owner_base + kind_index * LAYERS
        owner = (dp_place >= first_owner) & (dp_place < first_owner + LAYERS)
        ortho = lax.cond(owner, newton_schulz, blank_matrix, flat).reshape(whole.shape)
        width = selected[kind_index].shape[split_dim]
        own_shards.append(
            lax.dynamic_slice_in_dim(ortho, tensor_place * width, width, axis=split_dim)
        )
        scales.append(MUON_RATE * max(1.0, flat.shape[0] / flat.shape[1]) ** 0.5)
    updates = []
    for kind_index in range(4):
        layer_pieces = []
        for layer_index in range(LAYERS):
            layer_pieces.append(
                from_root(
                    shortened_2(own_shards[kind_index]),
                    "dp",
                    owner_base + kind_index * LAYERS + layer_index,
                )
            )
        updates.append(jnp.stack(layer_pieces))
    new_weights = [
        kinds[kind_index][0] * (1.0 - MUON_DECAY) - scales[kind_index] * updates[kind_index]
        for kind_index in range(4)
    ]
    emb_a, emb_b, emb_w = adam_update(
        embedding, embedding_first, embedding_second, grad_embed * factor, 0.5, 0.1
    )
    head_a, head_b, head_w = adam_update(
        head, head_first, head_second, grad_head * factor, 0.05, 0.1
    )
    gain_a, gain_b, gain_w = adam_update(
        gains, gains_first, gains_second, grad_gains * factor, 0.6, 0.0
    )
    bias_a, bias_b, bias_w = adam_update(
        up_bias, bias_first, bias_second, grad_bias * factor, 0.3, 0.0
    )
    bound_a, bound_b, bound_w = adam_update(
        boundary_weight, boundary_first, boundary_second, grad_bound * factor, 0.05, 0.0
    )
    return (
        loss_sum,
        count_total,
        grad_norm,
        new_moments[0],
        new_weights[0],
        new_moments[1],
        new_weights[1],
        new_moments[2],
        new_weights[2],
        new_moments[3],
        new_weights[3],
        emb_a,
        emb_b,
        emb_w,
        head_a,
        head_b,
        head_w,
        gain_a,
        gain_b,
        gain_w,
        bias_a,
        bias_b,
        bias_w,
        bound_a,
        bound_b,
        bound_w,
    )


def solution(mesh):
    return jax.shard_map(
        body,
        mesh=mesh,
        in_specs=(
            P("dp", None),
            P("dp", None),
            P("dp", None),
            P("dp"),
            P(),
            P(),
            P(None, None, None, "tensor"),
            P(None, "tensor", None),
            P(None, None, "tensor"),
            P(None, "tensor"),
            P(None, "tensor", None),
            P(),
            P(),
            P(None, None, None, "tensor"),
            P(None, "tensor", None),
            P(None, None, "tensor"),
            P(None, "tensor", None),
            P(),
            P(),
            P(),
            P(),
            P(),
            P(),
            P(None, "tensor"),
            P(None, "tensor"),
            P(),
            P(),
        ),
        out_specs=(
            P(),
            P(),
            P(),
            P(None, None, None, "tensor"),
            P(None, None, None, "tensor"),
            P(None, "tensor", None),
            P(None, "tensor", None),
            P(None, None, "tensor"),
            P(None, None, "tensor"),
            P(None, "tensor", None),
            P(None, "tensor", None),
            P(),
            P(),
            P(),
            P(),
            P(),
            P(),
            P(),
            P(),
            P(),
            P(None, "tensor"),
            P(None, "tensor"),
            P(None, "tensor"),
            P(),
            P(),
            P(),
        ),
        check_vma=False,
    )
```

profile of v0, /device:TPU:0, one launch (start us, length us, event | category | flops | bytes accessed | tf_op | source)
XLA Modules:
  0.0 1885.1 jit_solution(966683247367876439)
XLA Ops:
  94.8 55.6 %all-reduce.19.cloned.1.call-done = bf16[2048,512]{1,0:T(8,128)(2,1)} async-done(((bf16[2048,512]{1,0:T(8,128)(2,1)}), bf16[2048,512]{1,0:T(8,128)(2,1)}) %all-reduce.19.cloned.1.call-update) | async-done | bytes 2097168 | tf_op jit(solution)/shard_map/psum | solution.py:137
  171.9 60.6 %all-reduce.21.cloned.1.call-done = bf16[2048,512]{1,0:T(8,128)(2,1)} async-done(((bf16[2048,512]{1,0:T(8,128)(2,1)}), bf16[2048,512]{1,0:T(8,128)(2,1)}) %all-reduce.21.cloned.1.call-update) | async-done | bytes 2097168 | tf_op jit(solution)/shard_map/psum | solution.py:146
  250.8 24.4 %all-reduce.23.cloned.1.call-done = bf16[320,512]{1,0:T(8,128)(2,1)} async-done(((bf16[320,512]{1,0:T(8,128)(2,1)}), bf16[320,512]{1,0:T(8,128)(2,1)}) %all-reduce.23.cloned.1.call-update) | async-done | bytes 327696 | tf_op jit(solution)/shard_map/psum | solution.py:137
  282.6 24.4 %all-reduce.25.cloned.1.call-done = bf16[320,512]{1,0:T(8,128)(2,1)} async-done(((bf16[320,512]{1,0:T(8,128)(2,1)}), bf16[320,512]{1,0:T(8,128)(2,1)}) %all-reduce.25.cloned.1.call-update) | async-done | bytes 327696 | tf_op jit(solution)/shard_map/psum | solution.py:146
  394.7 63.2 %all-reduce.27.cloned.1.call-done = bf16[2048,512]{1,0:T(8,128)(2,1)} async-done(((bf16[2048,512]{1,0:T(8,128)(2,1)}), bf16[2048,512]{1,0:T(8,128)(2,1)}) %all-reduce.27.cloned.1.call-update) | async-done | bytes 2097168 | tf_op jit(solution)/shard_map/psum | solution.py:137
  484.0 56.3 %all-reduce.29.cloned.1.call-done = bf16[2048,512]{1,0:T(8,128)(2,1)} async-done(((bf16[2048,512]{1,0:T(8,128)(2,1)}), bf16[2048,512]{1,0:T(8,128)(2,1)}) %all-reduce.29.cloned.1.call-update) | async-done | bytes 2097168 | tf_op jit(solution)/shard_map/psum | solution.py:146
  547.5 34.0 %all-reduce = (f32[]{:T(128)}, f32[]{:T(128)}, f32[]{:T(128)}) all-reduce(f32[]{:T(128)S(6)} %neg.9, f32[]{:T(128)} %convert_reduce_fusion.1, f32[]{:T(128)} %get-tuple-element.60), channel_id=1, replica_groups=mesh['dp'=16,'tensor'=2] {'dp'}, use_global_device_ids=true, to_apply=%region_30.31 | all-reduce | flops 3 | bytes 24 | tf_op jit(solution)/shard_map/psum | solution.py:311
  613.1 59.1 %all-reduce.31.cloned.1.call-done = bf16[2048,512]{1,0:T(8,128)(2,1)} async-done(((bf16[2048,512]{1,0:T(8,128)(2,1)}), bf16[2048,512]{1,0:T(8,128)(2,1)}) %all-reduce.31.cloned.1.call-update) | async-done | bytes 2097168 | tf_op jit(solution)/shard_map/psum | solution.py:171
  691.6 15.5 multiply_reduce_fusion.7
  739.1 14.1 multiply_reduce_fusion.6
  766.7 11.7 multiply_convert_fusion.2
  810.7 55.1 %all-reduce.33.cloned.1.call-done = bf16[2048,512]{1,0:T(8,128)(2,1)} async-done(((bf16[2048,512]{1,0:T(8,128)(2,1)}), bf16[2048,512]{1,0:T(8,128)(2,1)}) %all-reduce.33.cloned.1.call-update) | async-done | bytes 2097168 | tf_op jit(solution)/shard_map/psum | solution.py:196
  888.7 17.5 all-reduce.35.cloned.1.call-done
  931.6 19.8 %all-reduce.37.cloned.1.call-done = bf16[320,512]{1,0:T(8,128)(2,1)} async-done(((bf16[320,512]{1,0:T(8,128)(2,1)}), bf16[320,512]{1,0:T(8,128)(2,1)}) %all-reduce.37.cloned.1.call-update) | async-done | bytes 327696 | tf_op jit(solution)/shard_map/psum | solution.py:196
  994.9 45.3 %all-reduce.39.cloned.1.call-done = bf16[2048,512]{1,0:T(8,128)(2,1)} async-done(((bf16[2048,512]{1,0:T(8,128)(2,1)}), bf16[2048,512]{1,0:T(8,128)(2,1)}) %all-reduce.39.cloned.1.call-update) | async-done | bytes 2097168 | tf_op jit(solution)/shard_map/psum | solution.py:171
  1057.7 15.3 multiply_reduce_fusion.5
  1104.4 13.9 multiply_reduce_fusion.4
  1131.9 11.7 multiply_convert_fusion
  1183.8 46.6 %all-reduce.41.cloned.1.call-done = bf16[2048,512]{1,0:T(8,128)(2,1)} async-done(((bf16[2048,512]{1,0:T(8,128)(2,1)}), bf16[2048,512]{1,0:T(8,128)(2,1)}) %all-reduce.41.cloned.1.call-update) | async-done | bytes 2097168 | tf_op jit(solution)/shard_map/psum | solution.py:196
  1248.2 65.0 %all-reduce.1 = (bf16[3,1024]{1,0:T(4,128)(2,1)S(1)}, bf16[1,512]{1,0:T(2,128)(2,1)S(1)}, bf16[6,512]{1,0:T(8,128)(2,1)S(1)}, bf16[512]{0:T(512)(128)(2,1)S(1)}) all-reduce(bf16[3,1024]{1,0:T(4,128)(2,1)S(1)} %pad_maximum_fusion.8, bf16[1,512]{1,0:T(2,128)(2,1)S(1)} %broadcast_in_dim.166, ...), channel_id=1, replica_groups=mesh['dp'=16,'tensor'=2] {'dp'}, use_global_device_ids=true, to_apply=%region_60.61 | all-reduce | flops 7168 | bytes 28672 | tf_op jit(solution)/shard_map/psum | solution.py:363
  1315.1 123.1 %all-reduce.45.cloned.1.call-done = (bf16[3,512,3,256]{3,1,2,0:T(8,128)(2,1)}, bf16[3,256,512]{2,1,0:T(8,128)(2,1)}, bf16[3,512,1024]{2,1,0:T(8,128)(2,1)}, bf16...) async-done(((bf16[3,512,3,256]{3,1,2,0:T(8,128)(2,1)}, bf16[3,256,512]{2,1,0:T(8,128)(2,1)}, bf16[3,512,1024]{2,1,0:T(8,128)(2,1)}, ...) | async-done | bytes 9961488 | tf_op jit(solution)/shard_map/psum | solution.py:360
  1487.2 14.8 all-gather.1
  1552.7 19.4 %all-gather.10.cloned.1.call-done = bf16[1,512,2048]{2,1,0:T(8,128)(2,1)} async-done(((bf16[1,512,1024]{2,1,0:T(8,128)(2,1)}), bf16[1,512,2048]{2,1,0:T(8,128)(2,1)}) %all-gather.10.cloned.1.call-update) | async-done | bytes 2097168 | tf_op jit(solution)/shard_map/all_gather | solution.py:420
  1596.2 262.0 %all-reduce.43.cloned.1.call-done = (bf16[1,512,3,256]{3,1,2,0:T(8,128)(2,1)}, bf16[1,512,3,256]{3,1,2,0:T(8,128)(2,1)}, bf16[1,512,3,256]{3,1,2,0:T(8,128)(2,1)...) async-done(((bf16[1,512,3,256]{3,1,2,0:T(8,128)(2,1)}, ...) | async-done | bytes 9437200 | tf_op jit(solution)/shard_map/psum | solution.py:35
  (837 shorter events, 722.0 us)
Async XLA Ops:
  7.2 143.1 %all-reduce.19.cloned.1.call-start = ((), (), s32[]{:S(2)}) async-start(), calls=%async_computation | async-start | bytes 4194304 | tf_op jit(solution)/shard_map/psum | solution.py:137
  9.7 144.1 %copy-start.193 = (f32[1,512]{1,0:T(1,128)}, f32[1,512]{1,0:T(1,128)S(1)}, u32[]{:S(2)}) copy-start(f32[1,512]{1,0:T(1,128)S(1)} %get-tuple-element.160) | copy-start | bytes 6148
  9.7 227.6 %copy-start.170 = (f32[1,512]{1,0:T(1,128)}, f32[1,512]{1,0:T(1,128)S(1)}, u32[]{:S(2)}) copy-start(f32[1,512]{1,0:T(1,128)S(1)} %get-tuple-element.159) | copy-start | bytes 6148
  9.7 266.7 %copy-start.172 = (f32[1,512]{1,0:T(1,128)}, f32[1,512]{1,0:T(1,128)S(1)}, u32[]{:S(2)}) copy-start(f32[1,512]{1,0:T(1,128)S(1)} %get-tuple-element.158) | copy-start | bytes 6148
  9.7 301.0 %copy-start.187 = (f32[1,512]{1,0:T(1,128)}, f32[1,512]{1,0:T(1,128)S(1)}, u32[]{:S(2)}) copy-start(f32[1,512]{1,0:T(1,128)S(1)} %get-tuple-element.157) | copy-start | bytes 6148
  84.3 148.2 %all-reduce.21.cloned.1.call-start = ((), (), s32[]{:S(2)}) async-start(), calls=%async_computation.1 | async-start | bytes 4194304 | tf_op jit(solution)/shard_map/psum | solution.py:146
  169.4 105.8 %all-reduce.23.cloned.1.call-start = ((), (), s32[]{:S(2)}) async-start(), calls=%async_computation.2 | async-start | bytes 655360 | tf_op jit(solution)/shard_map/psum | solution.py:137
  250.8 56.3 %all-reduce.25.cloned.1.call-start = ((), (), s32[]{:S(2)}) async-start(), calls=%async_computation.3 | async-start | bytes 655360 | tf_op jit(solution)/shard_map/psum | solution.py:146
  282.6 175.3 %all-reduce.27.cloned.1.call-start = ((), (), s32[]{:S(2)}) async-start(), calls=%async_computation.4 | async-start | bytes 4194304 | tf_op jit(solution)/shard_map/psum | solution.py:137
  358.9 332.6 %copy-start.63 = (bf16[2,1024,1,4,64]{1,4,3,0,2:T(8,128)(2,1)}, bf16[2,1024,1,4,64]{1,4,3,0,2:T(8,128)(2,1)S(1)}, u32[]{:S(2)}) copy-start(bf16[2,1024,1,4,64]{1,4,3,0,2:T(8,128)(2,1)S(1)} %copy.244) | copy-start | bytes 3145732
  394.7 145.6 %all-reduce.29.cloned.1.call-start = ((), (), s32[]{:S(2)}) async-start(), calls=%async_computation.5 | async-start | bytes 4194304 | tf_op jit(solution)/shard_map/psum | solution.py:146
  461.4 215.5 %copy-start.149 = (f32[2048]{0:T(1024)}, f32[2048]{0:T(1024)S(1)}, u32[]{:S(2)}) copy-start(f32[2048]{0:T(1024)S(1)} %fusion.298) | copy-start | bytes 24580
  477.1 195.1 %all-reduce.31.cloned.1.call-start = ((), (), s32[]{:S(2)}) async-start(), calls=%async_computation.6 | async-start | bytes 4194304 | tf_op jit(solution)/shard_map/psum | solution.py:171
  612.9 253.0 %all-reduce.33.cloned.1.call-start = ((), (), s32[]{:S(2)}) async-start(), calls=%async_computation.7 | async-start | bytes 4194304 | tf_op jit(solution)/shard_map/psum | solution.py:196
  803.0 103.3 %all-reduce.35.cloned.1.call-start = ((), (), s32[]{:S(2)}) async-start(), calls=%async_computation.8 | async-start | bytes 655360 | tf_op jit(solution)/shard_map/psum | solution.py:171
  881.8 69.7 %all-reduce.37.cloned.1.call-start = ((), (), s32[]{:S(2)}) async-start(), calls=%async_computation.9 | async-start | bytes 655360 | tf_op jit(solution)/shard_map/psum | solution.py:196
  927.0 113.2 %all-reduce.39.cloned.1.call-start = ((), (), s32[]{:S(2)}) async-start(), calls=%async_computation.10 | async-start | bytes 4194304 | tf_op jit(solution)/shard_map/psum | solution.py:171
  977.1 253.3 %all-reduce.41.cloned.1.call-start = ((), (), s32[]{:S(2)}) async-start(), calls=%async_computation.11 | async-start | bytes 4194304 | tf_op jit(solution)/shard_map/psum | solution.py:196
  1167.6 270.5 %all-reduce.45.cloned.1.call-start = ((), (), s32[]{:S(2)}) async-start(), calls=%async_computation.16 | async-start | bytes 19922944 | tf_op jit(solution)/shard_map/psum | solution.py:360
  1241.9 284.4 %all-gather.8.cloned.1.call-start = ((), (), s32[]{:S(2)}) async-start(), calls=%async_computation.12 | async-start | bytes 2359296 | tf_op jit(solution)/shard_map/all_gather | solution.py:414
  1469.4 71.3 %all-gather.12.cloned.1.call-start = ((), (), s32[]{:S(2)}) async-start(), calls=%async_computation.14 | async-start | bytes 3145728 | tf_op jit(solution)/shard_map/all_gather | solution.py:423
  1483.9 88.2 %all-gather.10.cloned.1.call-start = ((), (), s32[]{:S(2)}) async-start(), calls=%async_computation.13 | async-start | bytes 3145728 | tf_op jit(solution)/shard_map/all_gather | solution.py:420
  1516.0 342.2 %all-reduce.43.cloned.1.call-start = ((), (), s32[]{:S(2)}) async-start(), calls=%async_computation.15 | async-start | bytes 18874368 | tf_op jit(solution)/shard_map/psum | solution.py:35
  1585.0 273.2 %copy-start.47 = (f32[3,256,512]{2,1,0:T(8,128)S(1)}, f32[3,256,512]{2,1,0:T(8,128)}, u32[]{:S(2)}) copy-start(f32[3,256,512]{2,1,0:T(8,128)} %param.42) | copy-start | bytes 4718596
  (250 other events, 3138.1 us)
Sparse Core Ops, SparseCore 0:
  84.4 65.8 all-reduce.18
  169.5 62.9 all-reduce.20
  250.9 24.2 all-reduce.22
  282.7 24.2 all-reduce.24
  394.8 63.0 all-reduce.26
  477.2 62.9 all-reduce.28
  613.0 59.2 all-reduce.30
  803.1 62.7 all-reduce.32
  881.9 24.2 all-reduce.34
  927.1 24.2 all-reduce.36
  977.2 62.8 all-reduce.38
  1167.7 62.6 all-reduce.40
  1241.9 196.1 all-reduce.44
  1469.6 32.6 all-gather.7
  1504.3 33.1 all-gather.11
  1538.9 33.1 all-gather.9
  1585.1 273.0 all-reduce.42
where the time goes:
time: 1890 us
  waiting for transfers between devices  933 us (49%)
  matrix products  342 us (18%)
  other arithmetic  247 us (13%)
  local copies, waits for them, and re-layouts  183 us (10%)
  blocking collectives  119 us (6%)
  between operations  37.5 us (2%)
  loops' own time  22.6 us (1%)
    psum x1, waiting for transfers between devices, from_root(): return lax.psum(kept, axis)  262 us
    psum x3, waiting for transfers between devices, layer_forward(): lax.psum(partial_attn.astype(jnp.bfloat16), 'tensor').astype(jnp.float32)  143 us
    psum x3, waiting for transfers between devices, layer_forward(): lax.psum(partial_ffn.astype(jnp.bfloat16), 'tensor').astype(jnp.float32)  141 us
    psum x1, waiting for transfers between devices, body(): lax.psum(stacked[1].astype(jnp.bfloat16), 'dp').astype(jnp.float32)  123 us
    psum x3, waiting for transfers between devices, layer_backward(): lax.psum(partial_ffn.astype(jnp.bfloat16), 'tensor').astype(jnp.float32)  122 us
    psum x3, waiting for transfers between devices, layer_backward(): lax.psum(partial_attn.astype(jnp.bfloat16), 'tensor').astype(jnp.float32)  122 us
    unnamed x538, local copies, waits for them, and re-layouts  88.8 us
    psum x1, blocking collectives, body(): lax.psum(stacked[4].astype(jnp.bfloat16), 'dp').astype(jnp.float32)  65 us
  transfers between devices with their start and end apart: 17, of which 15 were waited for; matrix products, arithmetic and copies ran while one was open for 7% of the time, Pallas kernels for 0%

commit v1 on v0

--- a/solution.py
+++ b/solution.py
@@ -3,6 +3,7 @@
 import jax
 import jax.numpy as jnp
 from jax import lax
+from jax.sharding import Mesh
 from jax.sharding import PartitionSpec as P
 
 HEAD_SIZE = 64
@@ -499,66 +500,418 @@
     )
 
 
+BF = jnp.bfloat16
+F32 = jnp.float32
+SWAP = [(0, 1), (1, 0)]
+DP_AXES = ("zh", "zl", "y", "core")
+HALF_AXES = ("zl", "y", "core", "tensor")
+SPLIT_DIMS = (2, 0, 1, 0)
+
+
+def swap(value, axis):
+    return lax.ppermute(value, axis, SWAP)
+
+
+def summed_over(value, axes):
+    for axis in axes:
+        value = value + swap(value, axis)
+    return value
+
+
+def tie(values, *tokens):
+    return list(lax.optimization_barrier(tuple(values) + tokens)[: len(values)])
+
+
+def ordered(shard, mine, other, dim):
+    return jnp.where(
+        shard == 0, jnp.concatenate([mine, other], dim), jnp.concatenate([other, mine], dim)
+    )
+
+
+def exchange_weights(packed, core):
+    half = packed.shape[0] // 2
+    first = swap(lax.dynamic_slice_in_dim(packed, core * half, half, 0), "tensor")
+    second = swap(first, "core")
+    return jnp.where(core == 0, jnp.concatenate([first, second]), jnp.concatenate([second, first]))
+
+
+def attend_local(queries, key_rows, value_rows):
+    total = queries.shape[1]
+    step = 256 if total % 256 == 0 else total
+    outputs, summaries = [], []
+    for first in range(0, total, step):
+        last = first + step
+        scores = (
+            jnp.einsum(
+                "hqd,hkd->hqk", queries[:, first:last], key_rows[:, :last], preferred_element_type=F32
+            )
+            * HEAD_SIZE**-0.5
+        )
+        allowed = (first + jnp.arange(step))[:, None] >= jnp.arange(last)[None, :]
+        scores = jnp.where(allowed, scores, -1e30)
+        highest = jnp.max(scores, axis=-1, keepdims=True)
+        expo = jnp.exp(scores - highest)
+        totals = jnp.sum(expo, axis=-1, keepdims=True)
+        soft = (expo / totals).astype(BF)
+        outputs.append(
+            jnp.einsum("hqk,hkd->hqd", soft, value_rows[:, :last], preferred_element_type=F32).astype(BF)
+        )
+        summaries.append(highest + jnp.log(totals))
+    return jnp.concatenate(outputs, axis=1), jnp.concatenate(summaries, axis=1)
+
+
+def attend_local_back(queries, key_rows, value_rows, grad_mixed, mixed, summary):
+    total = queries.shape[1]
+    step = 256 if total % 256 == 0 else total
+    scale = HEAD_SIZE**-0.5
+    centre = jnp.sum(grad_mixed.astype(F32) * mixed.astype(F32), axis=-1, keepdims=True)
+    grad_keys = jnp.zeros(key_rows.shape, F32)
+    grad_values = jnp.zeros(key_rows.shape, F32)
+    grad_queries = []
+    for first in range(0, total, step):
+        last = first + step
+        query_block = queries[:, first:last]
+        grad_block = grad_mixed[:, first:last]
+        scores = jnp.einsum("hqd,hkd->hqk", query_block, key_rows[:, :last], preferred_element_type=F32) * scale
+        allowed = (first + jnp.arange(step))[:, None] >= jnp.arange(last)[None, :]
+        soft = jnp.exp(jnp.where(allowed, scores, -1e30) - summary[:, first:last])
+        grad_soft = jnp.einsum("hqd,hkd->hqk", grad_block, value_rows[:, :last], preferred_element_type=F32)
+        grad_scores = (soft * (grad_soft - centre[:, first:last])).astype(BF)
+        grad_queries.append(
+            scale * jnp.einsum("hqk,hkd->hqd", grad_scores, key_rows[:, :last], preferred_element_type=F32)
+        )
+        new_keys = scale * jnp.einsum("hqk,hqd->hkd", grad_scores, query_block, preferred_element_type=F32)
+        new_values = jnp.einsum("hqk,hqd->hkd", soft.astype(BF), grad_block, preferred_element_type=F32)
+        pad = ((0, 0), (0, total - last), (0, 0))
+        grad_keys = grad_keys + jnp.pad(new_keys, pad)
+        grad_values = grad_values + jnp.pad(new_values, pad)
+    return jnp.concatenate(grad_queries, axis=1), grad_keys, grad_values
+
+
+def heads_first(rows):
+    return jnp.transpose(rows.reshape(rows.shape[0], -1, HEAD_SIZE), (1, 0, 2))
+
+
+def rows_first(values):
+    return jnp.transpose(values, (1, 0, 2)).reshape(values.shape[1], -1)
+
+
+def whole_layer_forward(inputs, weights):
+    gain_pair, w_qkv, w_out, w_up, b_up, w_down = weights
+    normed = rms_norm(inputs, gain_pair[0]).astype(BF)
+    packed = [
+        heads_first(jnp.dot(normed, w_qkv[part], preferred_element_type=F32).astype(BF)) for part in range(3)
+    ]
+    mixed, summary = attend_local(*packed)
+    after = inputs + jnp.dot(rows_first(mixed), w_out, preferred_element_type=F32)
+    normed_ffn = rms_norm(after, gain_pair[1]).astype(BF)
+    hidden = jnp.dot(normed_ffn, w_up, preferred_element_type=F32) + b_up
+    result = after + jnp.dot(jax.nn.gelu(hidden).astype(BF), w_down, preferred_element_type=F32)
+    return result, (inputs, after, packed, mixed, summary, hidden)
+
+
+def whole_layer_backward(grad_result, saved, weights):
+    gain_pair, w_qkv, w_out, w_up, b_up, w_down = weights
+    inputs, after, packed, mixed, summary, hidden = saved
+    grad_branch = grad_result.astype(BF)
+    activated, gelu_back = jax.vjp(jax.nn.gelu, hidden)
+    grad_down = jnp.dot(activated.astype(BF).T, grad_branch, preferred_element_type=F32)
+    grad_act = jnp.dot(grad_branch, w_down.T, preferred_element_type=F32)
+    grad_hidden = gelu_back(grad_act)[0].astype(BF)
+    grad_bias = jnp.sum(grad_hidden.astype(F32), axis=0)
+    normed_ffn, norm_back_two = jax.vjp(rms_norm, after, gain_pair[1])
+    grad_up = jnp.dot(normed_ffn.astype(BF).T, grad_hidden, preferred_element_type=F32)
+    grad_after_norm, grad_gain_two = norm_back_two(jnp.dot(grad_hidden, w_up.T, preferred_element_type=F32))
+    grad_after = grad_result + grad_after_norm
+    grad_attn = grad_after.astype(BF)
+    grad_out = jnp.dot(rows_first(mixed).T, grad_attn, preferred_element_type=F32)
+    grad_mixed = heads_first(jnp.dot(grad_attn, w_out.T, preferred_element_type=F32).astype(BF))
+    grad_parts = [
+        rows_first(part.astype(BF)) for part in attend_local_back(*packed, grad_mixed, mixed, summary)
+    ]
+    normed, norm_back_one = jax.vjp(rms_norm, inputs, gain_pair[0])
+    normed_low = normed.astype(BF)
+    grad_qkv = jnp.stack([jnp.dot(normed_low.T, part, preferred_element_type=F32) for part in grad_parts])
+    grad_normed = sum(
+        jnp.dot(part, w_qkv[at].T, preferred_element_type=F32) for at, part in enumerate(grad_parts)
+    )
+    grad_inputs_norm, grad_gain_one = norm_back_one(grad_normed)
+    grads = (jnp.stack([grad_gain_one, grad_gain_two]), grad_qkv, grad_out, grad_up, grad_bias, grad_down)
+    return grad_after + grad_inputs_norm, grads
+
+
+def shard_pair(shard, values, dim):
+    width = values.shape[dim] // 2
+    mine = lax.dynamic_slice_in_dim(values, shard * width, width, dim)
+    return mine, lax.dynamic_slice_in_dim(values, (1 - shard) * width, width, dim)
+
+
+def to_rows(qkv, out, up, down):
+    ups = [up[:, :512], up[:, 512:]]
+    qkvs = [qkv.reshape(768, 512)]
+    return jnp.concatenate([out, down] + ups + qkvs, axis=0)
+
+
+def from_rows(rows):
+    up = jnp.concatenate([rows[1280:1792], rows[1792:2304]], axis=1)
+    return rows[2304:3072].reshape(3, 512, 256), rows[0:256], up, rows[256:1280]
+
+
+def newton_map(gram):
+    inverse = 1.0 / (jnp.sqrt(jnp.trace(gram)) + 1e-07)
+    gram = gram * (inverse * inverse)
+    eye = jnp.eye(512, dtype=F32)
+    total = None
+    for index in range(5):
+        poly = COEF_A * eye + COEF_B * gram + COEF_C * matmul_exact(gram, gram)
+        total = poly if total is None else matmul_exact(total, poly)
+        if index < 4:
+            gram = matmul_exact(matmul_exact(gram, poly), poly)
+            gram = 0.5 * (gram + gram.T)
+    return (total * inverse).astype(BF)
+
+
+def gram_of(left, right, dims):
+    return lax.dot_general(left, right, (dims, ((), ())), preferred_element_type=F32)
+
+
+def sequence_body(
+    tokens, targets, boundaries, lengths, embedding, head, qkv_weight, out_weight, up_weight, up_bias,
+    down_weight, gains, boundary_weight, qkv_moment, out_moment, up_moment, down_moment, embedding_first,
+    embedding_second, head_first, head_second, gains_first, gains_second, bias_first, bias_second,
+    boundary_first, boundary_second,
+):
+    length = tokens.shape[1]
+    core, shard = lax.axis_index("core"), lax.axis_index("tensor")
+    place_y, place_zl = lax.axis_index("y"), lax.axis_index("zl")
+    own_length = lax.dynamic_index_in_dim(lengths, shard, 0, keepdims=False)
+    token_row = lax.dynamic_index_in_dim(tokens, shard, 0, keepdims=False)
+    target_row = lax.dynamic_index_in_dim(targets, shard, 0, keepdims=False)
+    bound_row = lax.dynamic_index_in_dim(boundaries, shard, 0, keepdims=False)
+    qkv_parts = jnp.transpose(qkv_weight, (0, 2, 1, 3))
+    vocab_ids = jnp.arange(VOCAB, dtype=jnp.int32)
+    target_hot = (target_row[:, None] == vocab_ids[None, :]).astype(F32)
+    counted = (jnp.arange(length, dtype=jnp.int32) < own_length).astype(F32)
+    segment = jnp.cumsum(bound_row) - bound_row
+    short_ids = jnp.arange(SHORT, dtype=jnp.int32)
+    pool_hot = (segment[None, :] == short_ids[:, None]).astype(BF)
+    lift_hot = (segment[:, None] - 1 == short_ids[None, :]).astype(BF)
+    sizes_seg = jnp.sum(pool_hot.astype(F32), axis=1, keepdims=True)
+
+    rows_own, rows_other = [], []
+    for layer in range(LAYERS):
+        packed = to_rows(
+            *[value[layer].astype(BF) for value in (qkv_parts, out_weight, up_weight, down_weight)]
+        )
+        if rows_other:
+            (packed,) = tie([packed], rows_other[-1])
+        rows_own.append(packed)
+        rows_other.append(exchange_weights(packed, core))
+    bias_other = swap(up_bias, "tensor")
+    bias_whole = ordered(shard, up_bias, bias_other, 1)
+
+    def layer_weights(layer):
+        mine, other = from_rows(rows_own[layer]), from_rows(rows_other[layer])
+        dims = (2, 0, 1, 0)
+        w_qkv, w_out, w_up, w_down = [
+            ordered(shard, own, far, dim) for own, far, dim in zip(mine, other, dims)
+        ]
+        return gains[2 * layer : 2 * layer + 2], w_qkv, w_out, w_up, bias_whole[layer], w_down
+
+    weights = [layer_weights(layer) for layer in range(LAYERS)]
+    wide = jnp.zeros((8, 128), F32)
+    count_total = summed_over(
+        jnp.sum(jnp.clip(lengths, 0, length)).astype(F32).reshape(1, 1) + wide, DP_AXES
+    )[0, 0]
+
+    token_hot = (token_row[:, None] == vocab_ids[None, :]).astype(BF)
+    table_high = embedding.astype(BF)
+    table_rest = embedding - table_high.astype(F32)
+    table_mid = table_rest.astype(BF)
+    table_low = (table_rest - table_mid.astype(F32)).astype(BF)
+    start_rows = sum(
+        jnp.dot(token_hot, part, preferred_element_type=F32) for part in (table_high, table_mid, table_low)
+    )
+    first_out, saved_one = whole_layer_forward(start_rows, weights[0])
+    bound_prob = jax.nn.sigmoid(jnp.sum(first_out * boundary_weight, axis=-1))
+    shortened = jnp.dot(pool_hot, first_out.astype(BF), preferred_element_type=F32) / sizes_seg
+    short_out, saved_two = whole_layer_forward(shortened, weights[1])
+    lifted = jnp.dot(lift_hot, short_out.astype(BF), preferred_element_type=F32)
+    final_out, saved_three = whole_layer_forward(first_out + lifted, weights[2])
+    bound_total = summed_over(jnp.sum(counted * bound_prob).reshape(1, 1) + wide, DP_AXES + ("tensor",))[0, 0]
+    final_norm, final_back = jax.vjp(rms_norm, final_out, gains[2 * LAYERS])
+    final_low = final_norm.astype(BF)
+    head_low = head.astype(BF)
+    logits = jnp.dot(final_low, head_low, preferred_element_type=F32)
+    highest = jnp.max(logits, axis=-1, keepdims=True)
+    log_probs = logits - highest - jnp.log(jnp.sum(jnp.exp(logits - highest), axis=-1, keepdims=True))
+    local_cross = -jnp.sum(counted * jnp.sum(target_hot * log_probs, axis=-1))
+    rest_count = count_total - bound_total
+    prior_nll = -(
+        lax.lgamma(count_total + 1.0)
+        - lax.lgamma(bound_total + 1.0)
+        - lax.lgamma(rest_count + 1.0)
+        + bound_total * math.log(PRIOR_RATE)
+        + rest_count * math.log(1.0 - PRIOR_RATE)
+    )
+    prior_slope = (
+        lax.digamma(bound_total + 1.0)
+        - lax.digamma(rest_count + 1.0)
+        - math.log(PRIOR_RATE)
+        + math.log(1.0 - PRIOR_RATE)
+    ) / count_total
+    grad_logits = ((jnp.exp(log_probs) - target_hot) * (counted / count_total)[:, None]).astype(BF)
+    grad_head = jnp.dot(final_low.T, grad_logits, preferred_element_type=F32)
+    grad_final, gain_final = final_back(jnp.dot(grad_logits, head_low.T, preferred_element_type=F32))
+
+    def reduce_layer(grads):
+        _, grad_qkv, grad_out, grad_up, _, grad_down = grads
+        pairs = [
+            shard_pair(shard, value.astype(BF), dim)
+            for value, dim in zip((grad_qkv, grad_out, grad_up, grad_down), SPLIT_DIMS)
+        ]
+        mine = to_rows(*[pair[0] for pair in pairs])
+        other = to_rows(*[pair[1] for pair in pairs])
+        half = mine.shape[0] // 2
+        kept = [lax.dynamic_slice_in_dim(value, core * half, half, 0) for value in (mine, other)]
+        sent = [lax.dynamic_slice_in_dim(value, (1 - core) * half, half, 0) for value in (mine, other)]
+        got = swap(jnp.stack(sent), "core")
+        send_x = (kept[1].astype(F32) + got[1].astype(F32)).astype(BF)
+        total = kept[0].astype(F32) + got[0].astype(F32) + swap(send_x, "tensor").astype(F32)
+        return total.astype(BF)
+
+    grad_merged, grads_three = whole_layer_backward(grad_final, saved_three, weights[2])
+    sums = [None, None, reduce_layer(grads_three)]
+    grad_short = jnp.dot(lift_hot.T, grad_merged.astype(BF), preferred_element_type=F32)
+    grad_pooled, grads_two = whole_layer_backward(grad_short, saved_two, weights[1])
+    sums[1] = reduce_layer(grads_two)
+    early = lax.psum(jnp.stack([sums[1], sums[2]]), ("zh", "zl", "y"))
+    pooled_low = (grad_pooled / sizes_seg).astype(BF)
+    prior_term = prior_slope * counted * bound_prob * (1.0 - bound_prob)
+    grad_first = (
+        grad_merged
+        + jnp.dot(pool_hot.T, pooled_low, preferred_element_type=F32)
+        + prior_term[:, None] * boundary_weight[None, :]
+    )
+    grad_bound = jnp.sum(prior_term[:, None] * first_out, axis=0)
+    grad_start, grads_one = whole_layer_backward(grad_first, saved_one, weights[0])
+    start_high = grad_start.astype(BF)
+    start_low = (grad_start - start_high.astype(F32)).astype(BF)
+    grad_embed = sum(jnp.dot(token_hot.T, part, preferred_element_type=F32) for part in (start_high, start_low))
+    sums[0] = reduce_layer(grads_one)
+    tables = jnp.concatenate([grad_embed.reshape(256, 512), grad_head.reshape(256, 512)], axis=0).astype(BF)
+    tables = (tables.astype(F32) + swap(tables, "tensor").astype(F32)).astype(BF)
+    tables = (tables.astype(F32) + swap(tables, "core").astype(F32)).astype(BF)
+    late = lax.psum(jnp.concatenate([sums[0], tables], axis=0), ("zh", "zl", "y"))
+    halves = [late[:1536], early[0], early[1]]
+    stacked = jnp.stack(halves)
+    other_halves = swap(stacked, "core")
+    rows = jnp.where(
+        core == 0,
+        jnp.concatenate([stacked, other_halves], axis=1),
+        jnp.concatenate([other_halves, stacked], axis=1),
+    )
+    grad_embed, grad_head = late[1536:1792].astype(F32), late[1792:2048].reshape(512, 256).astype(F32)
+    split = [from_rows(rows[layer]) for layer in range(LAYERS)]
+    grads = [jnp.stack([split[layer][kind] for layer in range(LAYERS)]).astype(F32) for kind in range(4)]
+
+    all_grads = (grads_one, grads_two, grads_three)
+    bias_pairs = jnp.stack([each[4] for each in all_grads])
+    vectors = jnp.concatenate(
+        [each[0] for each in all_grads]
+        + [gain_final[None, :], grad_bound[None, :], bias_pairs.reshape(12, 512)]
+        + [jnp.broadcast_to(local_cross.reshape(1, 1), (4, 512))],
+        axis=0,
+    )
+    vectors = summed_over(vectors, DP_AXES + ("tensor",))
+    grad_gains, grad_bound, both_biases = vectors[0:7], vectors[7], vectors[8:20].reshape(LAYERS, 2048)
+    loss_sum = vectors[20, 0] + prior_nll
+    grad_bias = lax.dynamic_slice_in_dim(both_biases, shard * 1024, 1024, 1)
+    shared_squares = (
+        jnp.sum(vectors[0:20] * vectors[0:20]) + jnp.sum(grad_embed * grad_embed) + jnp.sum(grad_head * grad_head)
+    )
+    split_squares = sum(jnp.sum(grad * grad) for grad in grads)
+    split_squares = summed_over(split_squares.reshape(1, 1) + wide, ("tensor",))[0, 0]
+    grad_norm = jnp.sqrt(split_squares + shared_squares)
+    factor = jnp.minimum(1.0, CLIP_NORM / (grad_norm + 1e-06))
+
+    moments = [jnp.transpose(qkv_moment, (0, 2, 1, 3)), out_moment, up_moment, down_moment]
+    new_moments = [MOMENTUM * moment + grad * factor for moment, grad in zip(moments, grads)]
+    blends = [
+        (grad * factor + MOMENTUM * new).astype(BF) for grad, new in zip(grads, new_moments)
+    ]
+    slot = jnp.minimum(((place_zl * 2 + place_y) * 2 + core) * 2 + shard, 4 * LAYERS - 1)
+    own_layer = slot // 4
+    chosen = [lax.dynamic_index_in_dim(blend, own_layer, 0, keepdims=False) for blend in blends]
+
+    def first_pair(values):
+        qkv, out, up, down = values
+        gram = sum(gram_of(qkv[part], qkv[part], ((1,), (1,))) for part in range(3))
+        return jnp.stack([gram, gram_of(out, out, ((0,), (0,)))])
+
+    def second_pair(values):
+        qkv, out, up, down = values
+        return jnp.stack([gram_of(up, up, ((1,), (1,))), gram_of(down, down, ((0,), (0,)))])
+
+    shares = lax.cond((slot // 2) % 2 == 0, first_pair, second_pair, chosen)
+    sent = swap(lax.dynamic_index_in_dim(shares, 1 - shard, 0, keepdims=False), "tensor")
+    kept = lax.dynamic_index_in_dim(shares, shard, 0, keepdims=False)
+    maps = lax.all_gather(newton_map(kept + sent), HALF_AXES, axis=0, tiled=False)
+    weights_in = [qkv_parts, out_weight, up_weight, down_weight]
+    new_weights = [[] for _ in range(4)]
+    for layer in range(LAYERS):
+        qkv, out, up, down = [blend[layer] for blend in blends]
+        at = 4 * layer
+        updates = [
+            jnp.stack([jnp.dot(maps[at], qkv[part], preferred_element_type=F32) for part in range(3)]),
+            jnp.dot(out, maps[at + 1], preferred_element_type=F32),
+            jnp.dot(maps[at + 2], up, preferred_element_type=F32),
+            2.0 * jnp.dot(down, maps[at + 3], preferred_element_type=F32),
+        ]
+        for kind in range(4):
+            new_weights[kind].append(
+                weights_in[kind][layer] * (1.0 - MUON_DECAY) - MUON_RATE * updates[kind]
+            )
+    new_weights = [jnp.stack(value) for value in new_weights]
+    new_moments[0] = jnp.transpose(new_moments[0], (0, 2, 1, 3))
+    new_weights[0] = jnp.transpose(new_weights[0], (0, 2, 1, 3))
+    muon = []
+    for new_moment, new_weight in zip(new_moments, new_weights):
+        muon += [new_moment, new_weight]
+    return (
+        loss_sum,
+        count_total,
+        grad_norm,
+        *muon,
+        *adam_update(embedding, embedding_first, embedding_second, grad_embed * factor, 0.5, 0.1),
+        *adam_update(head, head_first, head_second, grad_head * factor, 0.05, 0.1),
+        *adam_update(gains, gains_first, gains_second, grad_gains * factor, 0.6, 0.0),
+        *adam_update(up_bias, bias_first, bias_second, grad_bias * factor, 0.3, 0.0),
+        *adam_update(boundary_weight, boundary_first, boundary_second, grad_bound * factor, 0.05, 0.0),
+    )
+
+
+def sequence_specs(dp):
+    split = [P(None, None, None, "tensor"), P(None, "tensor", None), P(None, None, "tensor"), P(None, "tensor"), P(None, "tensor", None)]
+    ins = [P(dp, None)] * 3 + [P(dp), P(), P()] + split + [P(), P()]
+    ins += [split[0], split[1], split[2], split[4]] + [P()] * 6 + [split[3]] * 2 + [P()] * 2
+    outs = [P()] * 3
+    for kind in (0, 1, 2, 4):
+        outs += [split[kind]] * 2
+    outs += [P()] * 9 + [split[3]] * 3 + [P()] * 3
+    return tuple(ins), tuple(outs)
+
+
 def solution(mesh):
-    return jax.shard_map(
-        body,
-        mesh=mesh,
-        in_specs=(
-            P("dp", None),
-            P("dp", None),
-            P("dp", None),
-            P("dp"),
-            P(),
-            P(),
-            P(None, None, None, "tensor"),
-            P(None, "tensor", None),
-            P(None, None, "tensor"),
-            P(None, "tensor"),
-            P(None, "tensor", None),
-            P(),
-            P(),
-            P(None, None, None, "tensor"),
-            P(None, "tensor", None),
-            P(None, None, "tensor"),
-            P(None, "tensor", None),
-            P(),
-            P(),
-            P(),
-            P(),
-            P(),
-            P(),
-            P(None, "tensor"),
-            P(None, "tensor"),
-            P(),
-            P(),
-        ),
-        out_specs=(
-            P(),
-            P(),
-            P(),
-            P(None, None, None, "tensor"),
-            P(None, None, None, "tensor"),
-            P(None, "tensor", None),
-            P(None, "tensor", None),
-            P(None, None, "tensor"),
-            P(None, None, "tensor"),
-            P(None, "tensor", None),
-            P(None, "tensor", None),
-            P(),
-            P(),
-            P(),
-            P(),
-            P(),
-            P(),
-            P(),
-            P(),
-            P(),
-            P(None, "tensor"),
-            P(None, "tensor"),
-            P(None, "tensor"),
-            P(),
-            P(),
-            P(),
-        ),
-        check_vma=False,
-    )
+    def run(tokens, *rest):
+        dp, tensor = mesh.shape["dp"], mesh.shape["tensor"]
+        if (dp, tensor) == (16, 2) and tokens.shape[0] == tensor * dp:
+            parts = Mesh(mesh.devices.reshape(2, 2, 2, 2, 2), DP_AXES + ("tensor",))
+            ins, outs = sequence_specs(DP_AXES)
+            step = jax.shard_map(sequence_body, mesh=parts, in_specs=ins, out_specs=outs, check_vma=False)
+        else:
+            ins, outs = sequence_specs("dp")
+            step = jax.shard_map(body, mesh=mesh, in_specs=ins, out_specs=outs, check_vma=False)
+        return step(tokens, *rest)
+
+    return run

time: 1890 us -> 1060 us (0.56)
  waiting for transfers between devices: 933 us -> 400 us
  blocking collectives: 119 us -> 0 us
  other arithmetic: 247 us -> 144 us
  matrix products: 342 us -> 296 us
  local copies, waits for them, and re-layouts: 183 us -> 141 us
  starting transfers between devices: 1.67 us -> 28.7 us
  loops' own time: 22.6 us -> 0.21 us
    psum x14 -> x1, waiting for transfers between devices: 913 us -> 184 us  [sequence_body(): early = lax.psum(jnp.stack([sums[1], sums[2]]), ('zh', 'zl', 'y'))]
    ppermute x0 -> x32, waiting for transfers between devices: none -> 179 us  [swap(): return lax.ppermute(value, axis, SWAP)]
    psum x3 -> x0, blocking collectives: 104 us -> none  [the longest x1 65 us: body(): lax.psum(stacked[4].astype(jnp.bfloat16), 'dp').astype(jnp.float32)]
    dot_general x73 -> x141, matrix products: 323 us -> 245 us  [the longest x3 29.3 us: whole_layer_backward(): grad_act = jnp.dot(grad_branch, w_down.T, preferred_element_type=F32)]
    unnamed x538 -> x606, local copies, waits for them, and re-layouts: 88.8 us -> 34.8 us
    reduce_sum x30 -> x24, other arithmetic: 77.9 us -> 30.6 us  [the longest x9 11.4 us: attend_local(): totals = jnp.sum(expo, axis=-1, keepdims=True)]
    convert_element_type x19 -> x13, other arithmetic: 72.6 us -> 28.2 us  [the longest x4 21.4 us: sequence_body(): (grad * factor + MOMENTUM * new).astype(BF)]
    another operation x27 -> x11, local copies, waits for them, and re-layouts: 42.1 us -> 3.22 us  [the longest x1 1.66 us: sequence_body(): stacked = jnp.stack(halves)]
  transfers between devices with their start and end apart: 17 -> 34, of which waited for: 15 -> 20; matrix products, arithmetic and copies ran while one was open for 7% -> 14% of each run, Pallas kernels for 0% -> 0%
where the time goes in v1:
time: 1060 us; the launch traced here: 1050 us
  waiting for transfers between devices  400 us (38%)
  matrix products  296 us (28%)
  other arithmetic  144 us (14%)
  local copies, waits for them, and re-layouts  141 us (13%)
  between operations  38.6 us (4%)
  starting transfers between devices  28.7 us (3%)
    psum x1, waiting for transfers between devices, sequence_body(): early = lax.psum(jnp.stack([sums[1], sums[2]]), ('zh', 'zl', 'y'))  184 us
    ppermute x32, waiting for transfers between devices, swap(): return lax.ppermute(value, axis, SWAP)  179 us
    dot_general x17, matrix products, matmul_exact(): return jnp.dot(left, right, precision=lax.Precision.HIGHEST)  51.6 us
    all_gather x1, waiting for transfers between devices, sequence_body(): lax.all_gather(newton_map(kept + sent), HALF_AXES, axis=0, tiled=False)  36.9 us
    unnamed x606, local copies, waits for them, and re-layouts  34.8 us
    dot_general x3, matrix products, whole_layer_backward(): grad_act = jnp.dot(grad_branch, w_down.T, preferred_element_type=F32)  29.3 us
    ppermute x32, starting transfers between devices, swap(): return lax.ppermute(value, axis, SWAP)  28.5 us
    convert_element_type x4, other arithmetic, sequence_body(): (grad * factor + MOMENTUM * new).astype(BF)  21.4 us
  transfers between devices with their start and end apart: 34, of which 20 were waited for; matrix products, arithmetic and copies ran while one was open for 14% of the time, Pallas kernels for 0%

profile of v1, /device:TPU:0, one launch (start us, length us, event | category | flops | bytes accessed | tf_op | source)
XLA Modules:
  0.0 1048.0 jit_solution(5339425693113496514)
XLA Ops:
  58.8 13.1 %collective-permute-done = bf16[1536,512]{1,0:T(8,128)(2,1)} collective-permute-done((bf16[1536,512]{1,0:T(8,128)(2,1)}, bf16[1536,512]{1,0:T(8,128)(2,1)}, u32[]{:S(2)}, u32[]{:S(2)}) %collective-permute-start) | collective-permute-done | bytes 1572896 | tf_op jit(solution)/shard_map/ppermute | solution.py:512
  133.2 9.2 collective-permute-done.3
  207.5 7.9 collective-permute-done.5
  257.7 6.5 fusion.428
  264.2 9.5 multiply_reduce_fusion.14
  281.1 9.3 convolution_convert_fusion.1
  290.4 14.3 %convert_reduce_fusion = (f32[2048]{0:T(1024)}, bf16[1024,2048]{1,0:T(8,128)(2,1)}) fusion(f32[1024,2048]{1,0:T(8,128)} %fusion.428, f32[2048]{0:T(1024)} %bitcast.745, bf16[1024,512]{1,0:T(8,128)(2,1)S(1)} %copy-done.146, bf16[1024,512]{1,0:T(8,128)(2,1)S(1)} %copy-done.145, pred[]{:T(512)S(6)} %eq.103, f32[1024,512]{0,1:T(8,128)} %copy-done.39), kind=kOutput, calls=%fused_computation.43 | convolution fusion | flops 2205677568 | bytes 16793600 | tf_op jit(solution)/shard_map/dot_general | solution.py:619
  304.8 6.7 multiply_reduce_fusion.3
  374.4 5.5 convolution_convert_fusion.5
  380.0 10.6 %convert_reduce_fusion.1 = (f32[2048]{0:T(1024)}, bf16[1024,2048]{1,0:T(8,128)(2,1)S(1)}) fusion(f32[1024,2048]{1,0:T(8,128)S(1)} %bitcast.761, f32[2048]{0:T(1024)S(1)} %bitcast.743, bf16[1024,512]{1,0:T(8,128)(2,1)S(1)} %copy-done.140, bf16[1024,512]{1,0:T(8,128)(2,1)S(1)} %copy-done.126, pred[]{:T(512)S(6)} %eq.103, f32[1024,512]{0,1:T(8,128)S(1)} %multiply_add_fusion), kind=kOutput, calls=%fused_computation.44 | convolution fusion | flops 2205677568 | bytes 16793600 | tf_op jit(solution)/shard_map/dot_general | solution.py:619
  438.3 5.9 multiply_convert_fusion
  485.7 12.2 %collective-permute-done.23 = bf16[512,512]{1,0:T(8,128)(2,1)S(1)} collective-permute-done((bf16[512,512]{1,0:T(8,128)(2,1)S(1)}, bf16[512,512]{1,0:T(8,128)(2,1)S(1)}, u32[]{:S(2)}, u32[]{:S(2)}) %collective-permute-start.23) | collective-permute-done | bytes 524320 | tf_op jit(solution)/shard_map/ppermute | solution.py:512
  502.7 28.9 %collective-permute-done.22 = bf16[1536,512]{1,0:T(8,128)(2,1)S(1)} collective-permute-done((bf16[1536,512]{1,0:T(8,128)(2,1)S(1)}, bf16[1536,512]{1,0:T(8,128)(2,1)S(1)}, u32[]{:S(2)}, u32[]{:S(2)}) %collective-permute-start.22) | collective-permute-done | bytes 1572896 | tf_op jit(solution)/shard_map/ppermute | solution.py:512
  533.7 31.6 %collective-permute-done.26 = bf16[1536,512]{1,0:T(8,128)(2,1)S(1)} collective-permute-done((bf16[1536,512]{1,0:T(8,128)(2,1)S(1)}, bf16[1536,512]{1,0:T(8,128)(2,1)S(1)}, u32[]{:S(2)}, u32[]{:S(2)}) %collective-permute-start.26) | collective-permute-done | bytes 1572896 | tf_op jit(solution)/shard_map/ppermute | solution.py:512
  566.0 32.7 %collective-permute-done.28 = bf16[1536,512]{1,0:T(8,128)(2,1)S(1)} collective-permute-done((bf16[1536,512]{1,0:T(8,128)(2,1)S(1)}, bf16[1536,512]{1,0:T(8,128)(2,1)S(1)}, u32[]{:S(2)}, u32[]{:S(2)}) %collective-permute-start.28) | collective-permute-done | bytes 1572896 | tf_op jit(solution)/shard_map/ppermute | solution.py:512
  602.9 183.5 %all-reduce.15.cloned.1.call-done = (bf16[2,1536,512]{2,1,0:T(8,128)(2,1)}, bf16[2048,512]{1,0:T(8,128)(2,1)}) async-done(((bf16[2,1536,512]{2,1,0:T(8,128)(2,1)}, bf16[2048,512]{1,0:T(8,128)(2,1)}), (bf16[2,1536,512]{2,1,0:T(8,128)(2,1)}, bf16[2048,512]{1,0:T(8,128)(2,1)})) %all-reduce.15.cloned.1.call-update) | async-done | bytes 5242896 | tf_op jit(solution)/shard_map/psum | solution.py:788
  813.7 7.6 maximum_select_fusion
  848.5 6.4 fusion.36
  854.9 5.6 fusion.46
  860.5 6.5 fusion.37
  872.9 24.1 %collective-permute-done.31 = f32[512,512]{1,0:T(8,128)S(1)} collective-permute-done((f32[512,512]{1,0:T(8,128)S(1)}, f32[512,512]{1,0:T(8,128)S(1)}, u32[]{:S(2)}, u32[]{:S(2)}) %collective-permute-start.31) | collective-permute-done | bytes 1048608 | tf_op jit(solution)/shard_map/ppermute | solution.py:512
  912.3 5.5 fusion.136
  951.0 5.2 fusion.133
  973.4 36.9 %all-gather.3.cloned.1.call-done = bf16[8192,512]{1,0:T(8,128)(2,1)} async-done(((bf16[512,512]{1,0:T(8,128)(2,1)}), bf16[8192,512]{1,0:T(8,128)(2,1)}) %all-gather.3.cloned.1.call-update) | async-done | bytes 8388624 | tf_op jit(solution)/shard_map/all_gather | solution.py:859
  (1053 shorter events, 528.1 us)
Async XLA Ops:
  7.2 779.1 %all-reduce.15.cloned.1.call-start = ((), (), s32[]{:S(2)}) async-start(), calls=%async_computation.1 | async-start | bytes 10485760 | tf_op jit(solution)/shard_map/psum | solution.py:788
  9.8 62.9 %collective-permute-start.7 = (f32[8,128]{1,0:T(8,128)}, f32[8,128]{1,0:T(8,128)}, u32[]{:S(2)}, u32[]{:S(2)}) collective-permute-start(f32[8,128]{1,0:T(8,128)} %add.813), channel_id=1, source_target_pairs={{0,16},{16,0},{1,17},{17,1},{2,18},{18,2},{3,19},{19,3},{4,20},{20... | collective-permute-start | bytes 12296 | tf_op jit(solution)/shard_map/ppermute | solution.py:512
  13.8 67.4 %collective-permute-start.2 = (f32[3,1024]{1,0:T(4,128)}, f32[3,1024]{1,0:T(4,128)}, u32[]{:S(2)}, u32[]{:S(2)}) collective-permute-start(f32[3,1024]{1,0:T(4,128)} %param.38), channel_id=1, source_target_pairs={{0,1},{1,0},{2,3},{3,2},{4,5},{5,4},{6,7},{7,6},{8,9},{9,8},{10,11... | collective-permute-start | bytes 36872 | tf_op jit(solution)/shard_map/ppermute | solution.py:512
  36.1 35.9 %collective-permute-start = (bf16[1536,512]{1,0:T(8,128)(2,1)}, bf16[1536,512]{1,0:T(8,128)(2,1)}, u32[]{:S(2)}, u32[]{:S(2)}) collective-permute-start(bf16[1536,512]{1,0:T(8,128)(2,1)} %constant_dynamic-slice_fusion.10), channel_id=1, source_target_pairs={{0,1},{1,0},{2,3},{3,2},{4,5},{5,4},{6,7},{7,6},{8,9},{9,8},{10,11... | collective-permute-start | bytes 4718600 | tf_op jit(solution)/shard_map/ppermute | solution.py:512
  72.0 13.2 %collective-permute-start.1 = (bf16[1536,512]{1,0:T(8,128)(2,1)}, bf16[1536,512]{1,0:T(8,128)(2,1)}, u32[]{:S(2)}, u32[]{:S(2)}) collective-permute-start(bf16[1536,512]{1,0:T(8,128)(2,1)} %collective-permute-done), channel_id=1, source_target_pairs={{0,2},{2,0},{1,3},{3,1},{4,6},{6,4},{5,7},{7,5},{8,10},{10,8},{9,1... | collective-permute-start | bytes 4718600 | tf_op jit(solution)/shard_map/ppermute | solution.py:512
  105.4 37.0 %collective-permute-start.3 = (bf16[1536,512]{1,0:T(8,128)(2,1)S(1)}, bf16[1536,512]{1,0:T(8,128)(2,1)}, u32[]{:S(2)}, u32[]{:S(2)}) collective-permute-start(bf16[1536,512]{1,0:T(8,128)(2,1)S(1)} %constant_dynamic-slice_fusion.8), channel_id=1, source_target_pairs={{0,1},{1,0},{2,3},{3,2},{4,5},{5,4},{6,7},{7,6},{8,9},{9,8},{10,11... | collective-permute-start | bytes 4718600 | tf_op jit(solution)/shard_map/ppermute | solution.py:512
  130.4 12.0 %collective-permute-start.11 = (f32[8,128]{1,0:T(8,128)S(1)}, f32[8,128]{1,0:T(8,128)S(1)}, u32[]{:S(2)}, u32[]{:S(2)}) collective-permute-start(f32[8,128]{1,0:T(8,128)S(1)} %add.839), channel_id=1, source_target_pairs={{0,16},{16,0},{1,17},{17,1},{2,18},{18,2},{3,19},{19,3},{4,20},{20... | collective-permute-start | bytes 12296 | tf_op jit(solution)/shard_map/ppermute | solution.py:512
  142.4 21.8 %collective-permute-start.4 = (bf16[1536,512]{1,0:T(8,128)(2,1)}, bf16[1536,512]{1,0:T(8,128)(2,1)}, u32[]{:S(2)}, u32[]{:S(2)}) collective-permute-start(bf16[1536,512]{1,0:T(8,128)(2,1)} %collective-permute-done.3), channel_id=1, source_target_pairs={{0,2},{2,0},{1,3},{3,1},{4,6},{6,4},{5,7},{7,5},{8,10},{10,8},{9,1... | collective-permute-start | bytes 4718600 | tf_op jit(solution)/shard_map/ppermute | solution.py:512
  178.9 36.5 %collective-permute-start.5 = (bf16[1536,512]{1,0:T(8,128)(2,1)}, bf16[1536,512]{1,0:T(8,128)(2,1)}, u32[]{:S(2)}, u32[]{:S(2)}) collective-permute-start(bf16[1536,512]{1,0:T(8,128)(2,1)} %constant_dynamic-slice_fusion.7), channel_id=1, source_target_pairs={{0,1},{1,0},{2,3},{3,2},{4,5},{5,4},{6,7},{7,6},{8,9},{9,8},{10,11... | collective-permute-start | bytes 4718600 | tf_op jit(solution)/shard_map/ppermute | solution.py:512
  215.4 8.8 collective-permute-start.6
  466.6 18.1 %collective-permute-start.21 = (bf16[2,1536,512]{2,1,0:T(8,128)(2,1)S(1)}, bf16[2,1536,512]{2,1,0:T(8,128)(2,1)S(1)}, u32[]{:S(2)}, u32[]{:S(2)}) collective-permute-start(bf16[2,1536,512]{2,1,0:T(8,128)(2,1)S(1)} %pad_maximum_fusion.5), channel_id=1, source_target_pairs={{0,2},{2,0},{1,3},{3,1},{4,6},{6,4},{5,7},{7,5},{8,10},{10,8},{9,1... | collective-permute-start | bytes 9437192 | tf_op jit(solution)/shard_map/ppermute | solution.py:512
  472.2 25.9 %collective-permute-start.25 = (bf16[2,1536,512]{2,1,0:T(8,128)(2,1)}, bf16[2,1536,512]{2,1,0:T(8,128)(2,1)S(1)}, u32[]{:S(2)}, u32[]{:S(2)}) collective-permute-start(bf16[2,1536,512]{2,1,0:T(8,128)(2,1)} %pad_maximum_fusion.6), channel_id=1, source_target_pairs={{0,2},{2,0},{1,3},{3,1},{4,6},{6,4},{5,7},{7,5},{8,10},{10,8},{9,1... | collective-permute-start | bytes 9437192 | tf_op jit(solution)/shard_map/ppermute | solution.py:512
  477.5 22.7 %collective-permute-start.27 = (bf16[2,1536,512]{2,1,0:T(8,128)(2,1)}, bf16[2,1536,512]{2,1,0:T(8,128)(2,1)}, u32[]{:S(2)}, u32[]{:S(2)}) collective-permute-start(bf16[2,1536,512]{2,1,0:T(8,128)(2,1)} %pad_maximum_fusion.7), channel_id=1, source_target_pairs={{0,2},{2,0},{1,3},{3,1},{4,6},{6,4},{5,7},{7,5},{8,10},{10,8},{9,1... | collective-permute-start | bytes 9437192 | tf_op jit(solution)/shard_map/ppermute | solution.py:512
  483.1 14.8 %collective-permute-start.23 = (bf16[512,512]{1,0:T(8,128)(2,1)S(1)}, bf16[512,512]{1,0:T(8,128)(2,1)S(1)}, u32[]{:S(2)}, u32[]{:S(2)}) collective-permute-start(bf16[512,512]{1,0:T(8,128)(2,1)S(1)} %pad_maximum_fusion.20), channel_id=1, source_target_pairs={{0,1},{1,0},{2,3},{3,2},{4,5},{5,4},{6,7},{7,6},{8,9},{9,8},{10,11... | collective-permute-start | bytes 1572872 | tf_op jit(solution)/shard_map/ppermute | solution.py:512
  485.1 46.5 %collective-permute-start.22 = (bf16[1536,512]{1,0:T(8,128)(2,1)S(1)}, bf16[1536,512]{1,0:T(8,128)(2,1)S(1)}, u32[]{:S(2)}, u32[]{:S(2)}) collective-permute-start(bf16[1536,512]{1,0:T(8,128)(2,1)S(1)} %fusion.75), channel_id=1, source_target_pairs={{0,1},{1,0},{2,3},{3,2},{4,5},{5,4},{6,7},{7,6},{8,9},{9,8},{10,11... | collective-permute-start | bytes 4718600 | tf_op jit(solution)/shard_map/ppermute | solution.py:512
  498.1 4.6 collective-permute-start.24
  498.6 66.7 %collective-permute-start.26 = (bf16[1536,512]{1,0:T(8,128)(2,1)S(1)}, bf16[1536,512]{1,0:T(8,128)(2,1)S(1)}, u32[]{:S(2)}, u32[]{:S(2)}) collective-permute-start(bf16[1536,512]{1,0:T(8,128)(2,1)S(1)} %fusion.72), channel_id=1, source_target_pairs={{0,1},{1,0},{2,3},{3,2},{4,5},{5,4},{6,7},{7,6},{8,9},{9,8},{10,11... | collective-permute-start | bytes 4718600 | tf_op jit(solution)/shard_map/ppermute | solution.py:512
  502.0 96.6 %collective-permute-start.28 = (bf16[1536,512]{1,0:T(8,128)(2,1)S(1)}, bf16[1536,512]{1,0:T(8,128)(2,1)S(1)}, u32[]{:S(2)}, u32[]{:S(2)}) collective-permute-start(bf16[1536,512]{1,0:T(8,128)(2,1)S(1)} %fusion.69), channel_id=1, source_target_pairs={{0,1},{1,0},{2,3},{3,2},{4,5},{5,4},{6,7},{7,6},{8,9},{9,8},{10,11... | collective-permute-start | bytes 4718600 | tf_op jit(solution)/shard_map/ppermute | solution.py:512
  602.6 407.7 %all-gather.3.cloned.1.call-start = ((), (), s32[]{:S(2)}) async-start(), calls=%async_computation | async-start | bytes 8912896 | tf_op jit(solution)/shard_map/all_gather | solution.py:859
  791.4 22.2 %collective-permute-start.29 = (bf16[3,1536,512]{2,1,0:T(8,128)(2,1)}, bf16[3,1536,512]{2,1,0:T(8,128)(2,1)}, u32[]{:S(2)}, u32[]{:S(2)}) collective-permute-start(bf16[3,1536,512]{2,1,0:T(8,128)(2,1)} %pad_maximum_fusion.4), channel_id=1, source_target_pairs={{0,2},{2,0},{1,3},{3,1},{4,6},{6,4},{5,7},{7,5},{8,10},{10,8},{9,1... | collective-permute-start | bytes 14155784 | tf_op jit(solution)/shard_map/ppermute | solution.py:512
  794.2 5.0 collective-permute-start.16
  803.4 4.2 collective-permute-start.18
  838.9 5.3 collective-permute-start.30
  872.3 24.6 %collective-permute-start.31 = (f32[512,512]{1,0:T(8,128)S(1)}, f32[512,512]{1,0:T(8,128)S(1)}, u32[]{:S(2)}, u32[]{:S(2)}) collective-permute-start(f32[512,512]{1,0:T(8,128)S(1)} %dynamic-slice_bitcast_fusion.12), channel_id=1, source_target_pairs={{0,1},{1,0},{2,3},{3,2},{4,5},{5,4},{6,7},{7,6},{8,9},{9,8},{10,11... | collective-permute-start | bytes 3145736 | tf_op jit(solution)/shard_map/ppermute | solution.py:512
  (302 other events, 1956.0 us)
Sparse Core Ops, SparseCore 0:
  602.8 183.5 all-reduce.14
  959.1 51.1 all-gather.2

commit v2 on v1

--- a/solution.py
+++ b/solution.py
@@ -610,34 +610,38 @@
     return result, (inputs, after, packed, mixed, summary, hidden)
 
 
-def whole_layer_backward(grad_result, saved, weights):
-    gain_pair, w_qkv, w_out, w_up, b_up, w_down = weights
-    inputs, after, packed, mixed, summary, hidden = saved
+def hidden_backward(grad_result, saved, weights):
+    gain_pair, _, _, w_up, _, w_down = weights
+    after, hidden = saved[1], saved[5]
     grad_branch = grad_result.astype(BF)
     activated, gelu_back = jax.vjp(jax.nn.gelu, hidden)
     grad_down = jnp.dot(activated.astype(BF).T, grad_branch, preferred_element_type=F32)
     grad_act = jnp.dot(grad_branch, w_down.T, preferred_element_type=F32)
     grad_hidden = gelu_back(grad_act)[0].astype(BF)
     grad_bias = jnp.sum(grad_hidden.astype(F32), axis=0)
-    normed_ffn, norm_back_two = jax.vjp(rms_norm, after, gain_pair[1])
+    normed_ffn, norm_back = jax.vjp(rms_norm, after, gain_pair[1])
     grad_up = jnp.dot(normed_ffn.astype(BF).T, grad_hidden, preferred_element_type=F32)
-    grad_after_norm, grad_gain_two = norm_back_two(jnp.dot(grad_hidden, w_up.T, preferred_element_type=F32))
-    grad_after = grad_result + grad_after_norm
+    grad_norm, grad_gain = norm_back(jnp.dot(grad_hidden, w_up.T, preferred_element_type=F32))
+    return grad_result + grad_norm, grad_up, grad_bias, grad_down, grad_gain
+
+
+def attention_backward(grad_after, saved, weights):
+    gain_pair, w_qkv, w_out = weights[:3]
+    inputs, _, packed, mixed, summary, _ = saved
     grad_attn = grad_after.astype(BF)
     grad_out = jnp.dot(rows_first(mixed).T, grad_attn, preferred_element_type=F32)
     grad_mixed = heads_first(jnp.dot(grad_attn, w_out.T, preferred_element_type=F32).astype(BF))
     grad_parts = [
         rows_first(part.astype(BF)) for part in attend_local_back(*packed, grad_mixed, mixed, summary)
     ]
-    normed, norm_back_one = jax.vjp(rms_norm, inputs, gain_pair[0])
+    normed, norm_back = jax.vjp(rms_norm, inputs, gain_pair[0])
     normed_low = normed.astype(BF)
     grad_qkv = jnp.stack([jnp.dot(normed_low.T, part, preferred_element_type=F32) for part in grad_parts])
     grad_normed = sum(
         jnp.dot(part, w_qkv[at].T, preferred_element_type=F32) for at, part in enumerate(grad_parts)
     )
-    grad_inputs_norm, grad_gain_one = norm_back_one(grad_normed)
-    grads = (jnp.stack([grad_gain_one, grad_gain_two]), grad_qkv, grad_out, grad_up, grad_bias, grad_down)
-    return grad_after + grad_inputs_norm, grads
+    grad_norm, grad_gain = norm_back(grad_normed)
+    return grad_after + grad_norm, grad_qkv, grad_out, grad_gain
 
 
 def shard_pair(shard, values, dim):
@@ -764,62 +768,105 @@
     grad_head = jnp.dot(final_low.T, grad_logits, preferred_element_type=F32)
     grad_final, gain_final = final_back(jnp.dot(grad_logits, head_low.T, preferred_element_type=F32))
 
-    def reduce_layer(grads):
-        _, grad_qkv, grad_out, grad_up, _, grad_down = grads
-        pairs = [
-            shard_pair(shard, value.astype(BF), dim)
-            for value, dim in zip((grad_qkv, grad_out, grad_up, grad_down), SPLIT_DIMS)
-        ]
-        mine = to_rows(*[pair[0] for pair in pairs])
-        other = to_rows(*[pair[1] for pair in pairs])
+    def pack_pair(pack, *values):
+        pairs = [shard_pair(shard, value.astype(BF), dim) for value, dim in values]
+        return pack(*[pair[0] for pair in pairs]), pack(*[pair[1] for pair in pairs])
+
+    def pack_hidden(up, down):
+        return jnp.concatenate([down, up[:, :512], up[:, 512:]], axis=0)
+
+    def pack_attention(qkv, out):
+        return jnp.concatenate([out, qkv.reshape(768, 512)], axis=0)
+
+    def over_core(mine, other):
         half = mine.shape[0] // 2
         kept = [lax.dynamic_slice_in_dim(value, core * half, half, 0) for value in (mine, other)]
         sent = [lax.dynamic_slice_in_dim(value, (1 - core) * half, half, 0) for value in (mine, other)]
         got = swap(jnp.stack(sent), "core")
-        send_x = (kept[1].astype(F32) + got[1].astype(F32)).astype(BF)
-        total = kept[0].astype(F32) + got[0].astype(F32) + swap(send_x, "tensor").astype(F32)
-        return total.astype(BF)
-
-    grad_merged, grads_three = whole_layer_backward(grad_final, saved_three, weights[2])
-    sums = [None, None, reduce_layer(grads_three)]
+        return kept[0].astype(F32) + got[0].astype(F32), (kept[1].astype(F32) + got[1].astype(F32)).astype(BF)
+
+    grad_mid, up_three, bias_three, down_three, gain_three_b = hidden_backward(grad_final, saved_three, weights[2])
+    part_ffn_three, send_ffn_three = over_core(*pack_pair(pack_hidden, (up_three, 1), (down_three, 0)))
+    (grad_mid,) = tie([grad_mid], send_ffn_three)
+    got_ffn_three = swap(send_ffn_three, "tensor")
+    grad_merged, qkv_three, out_three, gain_three_a = attention_backward(grad_mid, saved_three, weights[2])
+    part_attn_three, send_attn_three = over_core(*pack_pair(pack_attention, (qkv_three, 2), (out_three, 0)))
+    (got_ffn_three,) = tie([got_ffn_three], grad_merged)
+    (grad_merged,) = tie([grad_merged], send_attn_three)
+    got_attn_three = swap(send_attn_three, "tensor")
     grad_short = jnp.dot(lift_hot.T, grad_merged.astype(BF), preferred_element_type=F32)
-    grad_pooled, grads_two = whole_layer_backward(grad_short, saved_two, weights[1])
-    sums[1] = reduce_layer(grads_two)
-    early = lax.psum(jnp.stack([sums[1], sums[2]]), ("zh", "zl", "y"))
+    grad_mid, up_two, bias_two, down_two, gain_two_b = hidden_backward(grad_short, saved_two, weights[1])
+    grad_pooled, qkv_two, out_two, gain_two_a = attention_backward(grad_mid, saved_two, weights[1])
+    (got_attn_three,) = tie([got_attn_three], grad_pooled)
+    sum_three = jnp.concatenate(
+        [
+            (part_ffn_three + got_ffn_three.astype(F32)).astype(BF),
+            (part_attn_three + got_attn_three.astype(F32)).astype(BF),
+        ],
+        axis=0,
+    )
+    total_three = lax.psum(sum_three, ("zh", "zl", "y"))
+    part_ffn_two, send_ffn_two = over_core(*pack_pair(pack_hidden, (up_two, 1), (down_two, 0)))
+    part_attn_two, send_attn_two = over_core(*pack_pair(pack_attention, (qkv_two, 2), (out_two, 0)))
+    send_two = jnp.concatenate([send_ffn_two, send_attn_two], axis=0)
+    part_two = jnp.concatenate([part_ffn_two, part_attn_two], axis=0)
+    got_two = swap(send_two, "tensor")
     pooled_low = (grad_pooled / sizes_seg).astype(BF)
     prior_term = prior_slope * counted * bound_prob * (1.0 - bound_prob)
+    (grad_merged,) = tie([grad_merged], sum_three, send_two)
     grad_first = (
         grad_merged
         + jnp.dot(pool_hot.T, pooled_low, preferred_element_type=F32)
         + prior_term[:, None] * boundary_weight[None, :]
     )
     grad_bound = jnp.sum(prior_term[:, None] * first_out, axis=0)
-    grad_start, grads_one = whole_layer_backward(grad_first, saved_one, weights[0])
+    grad_mid, up_one, bias_one, down_one, gain_one_b = hidden_backward(grad_first, saved_one, weights[0])
+    part_ffn_one, send_ffn_one = over_core(*pack_pair(pack_hidden, (up_one, 1), (down_one, 0)))
+    (got_two,) = tie([got_two], grad_mid)
+    sum_two = (part_two + got_two.astype(F32)).astype(BF)
+    total_two = lax.psum(sum_two, ("zh", "zl", "y"))
+    got_ffn_one = swap(send_ffn_one, "tensor")
+    (grad_mid,) = tie([grad_mid], sum_two, send_ffn_one)
+    grad_start, qkv_one, out_one, gain_one_a = attention_backward(grad_mid, saved_one, weights[0])
+    (got_ffn_one,) = tie([got_ffn_one], grad_start)
+    part_attn_one, send_attn_one = over_core(*pack_pair(pack_attention, (qkv_one, 2), (out_one, 0)))
+    got_attn_one = swap(send_attn_one, "tensor")
     start_high = grad_start.astype(BF)
     start_low = (grad_start - start_high.astype(F32)).astype(BF)
     grad_embed = sum(jnp.dot(token_hot.T, part, preferred_element_type=F32) for part in (start_high, start_low))
-    sums[0] = reduce_layer(grads_one)
     tables = jnp.concatenate([grad_embed.reshape(256, 512), grad_head.reshape(256, 512)], axis=0).astype(BF)
     tables = (tables.astype(F32) + swap(tables, "tensor").astype(F32)).astype(BF)
     tables = (tables.astype(F32) + swap(tables, "core").astype(F32)).astype(BF)
-    late = lax.psum(jnp.concatenate([sums[0], tables], axis=0), ("zh", "zl", "y"))
-    halves = [late[:1536], early[0], early[1]]
-    stacked = jnp.stack(halves)
+    late = lax.psum(
+        jnp.concatenate(
+            [
+                (part_ffn_one + got_ffn_one.astype(F32)).astype(BF),
+                (part_attn_one + got_attn_one.astype(F32)).astype(BF),
+                tables,
+            ],
+            axis=0,
+        ),
+        ("zh", "zl", "y"),
+    )
+    stacked = jnp.stack([late[:1536], total_two, total_three])
     other_halves = swap(stacked, "core")
-    rows = jnp.where(
-        core == 0,
-        jnp.concatenate([stacked, other_halves], axis=1),
-        jnp.concatenate([other_halves, stacked], axis=1),
-    )
+    low_half = jnp.where(core == 0, stacked, other_halves)
+    high_half = jnp.where(core == 0, other_halves, stacked)
+    hidden_rows = jnp.concatenate([low_half[:, :1024], high_half[:, :1024]], axis=1)
+    attention_rows = jnp.concatenate([low_half[:, 1024:], high_half[:, 1024:]], axis=1)
     grad_embed, grad_head = late[1536:1792].astype(F32), late[1792:2048].reshape(512, 256).astype(F32)
-    split = [from_rows(rows[layer]) for layer in range(LAYERS)]
-    grads = [jnp.stack([split[layer][kind] for layer in range(LAYERS)]).astype(F32) for kind in range(4)]
-
-    all_grads = (grads_one, grads_two, grads_three)
-    bias_pairs = jnp.stack([each[4] for each in all_grads])
+    grads = [
+        attention_rows[:, 256:].reshape(LAYERS, 3, 512, 256),
+        attention_rows[:, :256],
+        jnp.concatenate([hidden_rows[:, 1024:1536], hidden_rows[:, 1536:]], axis=2),
+        hidden_rows[:, :1024],
+    ]
+    grads = [value.astype(F32) for value in grads]
+
+    gain_rows = [gain_one_a, gain_one_b, gain_two_a, gain_two_b, gain_three_a, gain_three_b, gain_final, grad_bound]
+    bias_pairs = jnp.stack([bias_one, bias_two, bias_three])
     vectors = jnp.concatenate(
-        [each[0] for each in all_grads]
-        + [gain_final[None, :], grad_bound[None, :], bias_pairs.reshape(12, 512)]
+        [jnp.stack(gain_rows), bias_pairs.reshape(12, 512)]
         + [jnp.broadcast_to(local_cross.reshape(1, 1), (4, 512))],
         axis=0,
     )

time: 1060 us -> 960 us (0.906)
  waiting for transfers between devices: 400 us -> 326 us
  matrix products: 296 us -> 258 us
    ppermute x32 -> x37, waiting for transfers between devices: 179 us -> 104 us  [swap(): return lax.ppermute(value, axis, SWAP)]
    unnamed x606 -> x637, local copies, waits for them, and re-layouts: 34.8 us -> 45.2 us
    ppermute x32 -> x37, starting transfers between devices: 28.5 us -> 30.8 us  [swap(): return lax.ppermute(value, axis, SWAP)]
  transfers between devices with their start and end apart: 34 -> 39, of which waited for: 20 -> 20; matrix products, arithmetic and copies ran while one was open for 14% -> 29% of each run, Pallas kernels for 0% -> 0%
where the time goes in v2:
time: 960 us; the launch traced here: 952 us
  waiting for transfers between devices  326 us (34%)
  matrix products  258 us (27%)
  local copies, waits for them, and re-layouts  150 us (16%)
  other arithmetic  148 us (15%)
  between operations  39 us (4%)
  starting transfers between devices  30.9 us (3%)
    psum x1, waiting for transfers between devices, sequence_body(): total_three = lax.psum(sum_three, ('zh', 'zl', 'y'))  184 us
    ppermute x37, waiting for transfers between devices, swap(): return lax.ppermute(value, axis, SWAP)  104 us
    dot_general x17, matrix products, matmul_exact(): return jnp.dot(left, right, precision=lax.Precision.HIGHEST)  50.5 us
    unnamed x637, local copies, waits for them, and re-layouts  45.2 us
    all_gather x1, waiting for transfers between devices, sequence_body(): lax.all_gather(newton_map(kept + sent), HALF_AXES, axis=0, tiled=False)  37.1 us
    ppermute x37, starting transfers between devices, swap(): return lax.ppermute(value, axis, SWAP)  30.8 us
    dot_general x3, matrix products, hidden_backward(): grad_act = jnp.dot(grad_branch, w_down.T, preferred_element_type=F32)  28 us
    dot_general x9, matrix products, attend_local_back(): jnp.einsum('hqd,hkd->hqk', grad_block, value_rows[:, :last], preferred_el...  19.2 us
  transfers between devices with their start and end apart: 39, of which 20 were waited for; matrix products, arithmetic and copies ran while one was open for 29% of the time, Pallas kernels for 0%

profile of v2, /device:TPU:0, one launch (start us, length us, event | category | flops | bytes accessed | tf_op | source)
XLA Modules:
  0.0 951.7 jit_solution(13372166700435707305)
XLA Ops:
  20.4 4.8 fusion.186
  56.1 14.7 %collective-permute-done = bf16[1536,512]{1,0:T(8,128)(2,1)} collective-permute-done((bf16[1536,512]{1,0:T(8,128)(2,1)}, bf16[1536,512]{1,0:T(8,128)(2,1)}, u32[]{:S(2)}, u32[]{:S(2)}) %collective-permute-start) | collective-permute-done | bytes 1572896 | tf_op jit(solution)/shard_map/ppermute | solution.py:512
  131.8 9.3 collective-permute-done.3
  205.6 8.6 collective-permute-done.5
  214.1 4.3 multiply_reduce_fusion.16
  265.6 4.6 convolution_convert_fusion.5
  270.2 12.6 %convert_reduce_fusion = (f32[2048]{0:T(1024)}, bf16[1024,2048]{1,0:T(8,128)(2,1)S(1)}) fusion(f32[1024,2048]{1,0:T(8,128)} %copy-done.290, f32[2048]{0:T(1024)S(1)} %bitcast.780, bf16[1024,512]{1,0:T(8,128)(2,1)S(1)} %copy-done.164, bf16[1024,512]{1,0:T(8,128)(2,1)S(1)} %copy-done.163, pred[]{:T(512)S(6)} %eq.104, f32[1024,512]{0,1:T(8,128)S(1)} %add_add_fusion.4), kind=kOutput, calls=%fused_computation.42 | convolution fusion | flops 2205677568 | bytes 16793600 | tf_op jit(solution)/shard_map/dot_general | solution.py:619
  289.7 5.0 multiply_reduce_fusion.3
  357.7 4.8 convert_reduce_fusion.2
  391.5 8.1 convolution_convert_fusion.1
  399.6 10.6 %convert_reduce_fusion.1 = (f32[2048]{0:T(1024)}, bf16[1024,2048]{1,0:T(8,128)(2,1)S(1)}) fusion(f32[1024,2048]{1,0:T(8,128)S(1)} %bitcast.795, f32[2048]{0:T(1024)S(1)} %bitcast.777, bf16[1024,512]{1,0:T(8,128)(2,1)S(1)} %copy-done.155, bf16[1024,512]{1,0:T(8,128)(2,1)S(1)} %copy-done.141, pred[]{:T(512)S(6)} %eq.104, f32[1024,512]{0,1:T(8,128)S(1)} %multiply_add_fusion), kind=kOutput, calls=%fused_computation.43 | convolution fusion | flops 2205677568 | bytes 16793600 | tf_op jit(solution)/shard_map/dot_general | solution.py:619
  421.0 11.0 %collective-permute-done.22 = bf16[1536,512]{1,0:T(8,128)(2,1)S(1)} collective-permute-done((bf16[1536,512]{1,0:T(8,128)(2,1)S(1)}, bf16[1536,512]{1,0:T(8,128)(2,1)S(1)}, u32[]{:S(2)}, u32[]{:S(2)}) %collective-permute-start.22) | collective-permute-done | bytes 1572896 | tf_op jit(solution)/shard_map/ppermute | solution.py:512
  487.0 6.4 collective-permute-done.32
  498.6 11.1 %collective-permute-done.31 = bf16[512,512]{1,0:T(8,128)(2,1)S(1)} collective-permute-done((bf16[512,512]{1,0:T(8,128)(2,1)S(1)}, bf16[512,512]{1,0:T(8,128)(2,1)S(1)}, u32[]{:S(2)}, u32[]{:S(2)}) %collective-permute-start.31) | collective-permute-done | bytes 524320 | tf_op jit(solution)/shard_map/ppermute | solution.py:512
  511.7 184.0 %all-reduce.15.cloned.1.call-done = (bf16[1,1536,512]{2,1,0:T(8,128)(2,1)}, bf16[1,1536,512]{2,1,0:T(8,128)(2,1)}, bf16[2048,512]{1,0:T(8,128)(2,1)}) async-done(((bf16[1,1536,512]{2,1,0:T(8,128)(2,1)}, bf16[1,1536,512]{2,1,0:T(8,128)(2,1)}, bf16[2048,512]{1,0:T(8,128)(2,1)}), (bf16[1,1536,512]{2,1,0:T(8,128)(2,1)}, bf16[1,1536,512]{2,1,0:T(8,128)(2,1)}, ...) | async-done | bytes 5242896 | tf_op jit(solution)/shard_map/psum | solution.py:808
  748.3 6.1 mul.1540
  757.7 6.6 fusion.36
  780.7 23.4 %collective-permute-done.36 = f32[512,512]{1,0:T(8,128)S(1)} collective-permute-done((f32[512,512]{1,0:T(8,128)S(1)}, f32[512,512]{1,0:T(8,128)S(1)}, u32[]{:S(2)}, u32[]{:S(2)}) %collective-permute-start.36) | collective-permute-done | bytes 1048608 | tf_op jit(solution)/shard_map/ppermute | solution.py:512
  806.6 4.3 fusion.187
  818.1 5.0 fusion.130
  831.2 4.6 fusion.129
  843.8 4.6 fusion.128
  856.6 4.5 fusion.127
  878.4 37.1 %all-gather.3.cloned.1.call-done = bf16[8192,512]{1,0:T(8,128)(2,1)} async-done(((bf16[512,512]{1,0:T(8,128)(2,1)}), bf16[8192,512]{1,0:T(8,128)(2,1)}) %all-gather.3.cloned.1.call-update) | async-done | bytes 8388624 | tf_op jit(solution)/shard_map/all_gather | solution.py:906
  (1120 shorter events, 519.4 us)
Async XLA Ops:
  7.2 688.4 %all-reduce.15.cloned.1.call-start = ((), (), s32[]{:S(2)}) async-start(), calls=%async_computation.1 | async-start | bytes 10485760 | tf_op jit(solution)/shard_map/psum | solution.py:808
  9.8 61.8 %collective-permute-start.7 = (f32[8,128]{1,0:T(8,128)}, f32[8,128]{1,0:T(8,128)}, u32[]{:S(2)}, u32[]{:S(2)}) collective-permute-start(f32[8,128]{1,0:T(8,128)} %add.857), channel_id=1, source_target_pairs={{0,16},{16,0},{1,17},{17,1},{2,18},{18,2},{3,19},{19,3},{4,20},{20... | collective-permute-start | bytes 12296 | tf_op jit(solution)/shard_map/ppermute | solution.py:512
  13.8 66.3 %collective-permute-start.2 = (f32[3,1024]{1,0:T(4,128)}, f32[3,1024]{1,0:T(4,128)}, u32[]{:S(2)}, u32[]{:S(2)}) collective-permute-start(f32[3,1024]{1,0:T(4,128)} %param.38), channel_id=1, source_target_pairs={{0,1},{1,0},{2,3},{3,2},{4,5},{5,4},{6,7},{7,6},{8,9},{9,8},{10,11... | collective-permute-start | bytes 36872 | tf_op jit(solution)/shard_map/ppermute | solution.py:512
  34.9 35.9 %collective-permute-start = (bf16[1536,512]{1,0:T(8,128)(2,1)}, bf16[1536,512]{1,0:T(8,128)(2,1)}, u32[]{:S(2)}, u32[]{:S(2)}) collective-permute-start(bf16[1536,512]{1,0:T(8,128)(2,1)} %constant_dynamic-slice_fusion.35), channel_id=1, source_target_pairs={{0,1},{1,0},{2,3},{3,2},{4,5},{5,4},{6,7},{7,6},{8,9},{9,8},{10,11... | collective-permute-start | bytes 4718600 | tf_op jit(solution)/shard_map/ppermute | solution.py:512
  70.8 13.2 %collective-permute-start.1 = (bf16[1536,512]{1,0:T(8,128)(2,1)}, bf16[1536,512]{1,0:T(8,128)(2,1)}, u32[]{:S(2)}, u32[]{:S(2)}) collective-permute-start(bf16[1536,512]{1,0:T(8,128)(2,1)} %collective-permute-done), channel_id=1, source_target_pairs={{0,2},{2,0},{1,3},{3,1},{4,6},{6,4},{5,7},{7,5},{8,10},{10,8},{9,1... | collective-permute-start | bytes 4718600 | tf_op jit(solution)/shard_map/ppermute | solution.py:512
  104.2 37.0 %collective-permute-start.3 = (bf16[1536,512]{1,0:T(8,128)(2,1)S(1)}, bf16[1536,512]{1,0:T(8,128)(2,1)}, u32[]{:S(2)}, u32[]{:S(2)}) collective-permute-start(bf16[1536,512]{1,0:T(8,128)(2,1)S(1)} %constant_dynamic-slice_fusion.33), channel_id=1, source_target_pairs={{0,1},{1,0},{2,3},{3,2},{4,5},{5,4},{6,7},{7,6},{8,9},{9,8},{10,11... | collective-permute-start | bytes 4718600 | tf_op jit(solution)/shard_map/ppermute | solution.py:512
  129.6 11.5 %collective-permute-start.17 = (f32[8,128]{1,0:T(8,128)S(1)}, f32[8,128]{1,0:T(8,128)S(1)}, u32[]{:S(2)}, u32[]{:S(2)}) collective-permute-start(f32[8,128]{1,0:T(8,128)S(1)} %add.899), channel_id=1, source_target_pairs={{0,16},{16,0},{1,17},{17,1},{2,18},{18,2},{3,19},{19,3},{4,20},{20... | collective-permute-start | bytes 12296 | tf_op jit(solution)/shard_map/ppermute | solution.py:512
  141.1 21.8 %collective-permute-start.4 = (bf16[1536,512]{1,0:T(8,128)(2,1)}, bf16[1536,512]{1,0:T(8,128)(2,1)}, u32[]{:S(2)}, u32[]{:S(2)}) collective-permute-start(bf16[1536,512]{1,0:T(8,128)(2,1)} %collective-permute-done.3), channel_id=1, source_target_pairs={{0,2},{2,0},{1,3},{3,1},{4,6},{6,4},{5,7},{7,5},{8,10},{10,8},{9,1... | collective-permute-start | bytes 4718600 | tf_op jit(solution)/shard_map/ppermute | solution.py:512
  177.6 36.5 %collective-permute-start.5 = (bf16[1536,512]{1,0:T(8,128)(2,1)}, bf16[1536,512]{1,0:T(8,128)(2,1)}, u32[]{:S(2)}, u32[]{:S(2)}) collective-permute-start(bf16[1536,512]{1,0:T(8,128)(2,1)} %constant_dynamic-slice_fusion.32), channel_id=1, source_target_pairs={{0,1},{1,0},{2,3},{3,2},{4,5},{5,4},{6,7},{7,6},{8,9},{9,8},{10,11... | collective-permute-start | bytes 4718600 | tf_op jit(solution)/shard_map/ppermute | solution.py:512
  214.1 8.5 collective-permute-start.6
  289.3 15.7 %collective-permute-start.11 = (bf16[2,1024,512]{2,1,0:T(8,128)(2,1)}, bf16[2,1024,512]{2,1,0:T(8,128)(2,1)}, u32[]{:S(2)}, u32[]{:S(2)}) collective-permute-start(bf16[2,1024,512]{2,1,0:T(8,128)(2,1)} %pad_maximum_fusion.9), channel_id=1, source_target_pairs={{0,2},{2,0},{1,3},{3,1},{4,6},{6,4},{5,7},{7,5},{8,10},{10,8},{9,1... | collective-permute-start | bytes 6291464 | tf_op jit(solution)/shard_map/ppermute | solution.py:512
  318.4 65.8 %collective-permute-start.13 = (bf16[1024,512]{1,0:T(8,128)(2,1)}, bf16[1024,512]{1,0:T(8,128)(2,1)}, u32[]{:S(2)}, u32[]{:S(2)}) collective-permute-start(bf16[1024,512]{1,0:T(8,128)(2,1)} %fusion.93), channel_id=1, source_target_pairs={{0,1},{1,0},{2,3},{3,2},{4,5},{5,4},{6,7},{7,6},{8,9},{9,8},{10,11... | collective-permute-start | bytes 3145736 | tf_op jit(solution)/shard_map/ppermute | solution.py:512
  375.3 10.6 %collective-permute-start.15 = (bf16[2,1024,512]{2,1,0:T(8,128)(2,1)}, bf16[2,1024,512]{2,1,0:T(8,128)(2,1)}, u32[]{:S(2)}, u32[]{:S(2)}) collective-permute-start(bf16[2,1024,512]{2,1,0:T(8,128)(2,1)} %pad_maximum_fusion.12), channel_id=1, source_target_pairs={{0,2},{2,0},{1,3},{3,1},{4,6},{6,4},{5,7},{7,5},{8,10},{10,8},{9,1... | collective-permute-start | bytes 6291464 | tf_op jit(solution)/shard_map/ppermute | solution.py:512
  383.6 101.8 %collective-permute-start.14 = (bf16[512,512]{1,0:T(8,128)(2,1)}, bf16[512,512]{1,0:T(8,128)(2,1)}, u32[]{:S(2)}, u32[]{:S(2)}) collective-permute-start(bf16[512,512]{1,0:T(8,128)(2,1)} %fusion.194), channel_id=1, source_target_pairs={{0,1},{1,0},{2,3},{3,2},{4,5},{5,4},{6,7},{7,6},{8,9},{9,8},{10,11... | collective-permute-start | bytes 1572872 | tf_op jit(solution)/shard_map/ppermute | solution.py:512
  389.2 42.7 %collective-permute-start.22 = (bf16[1536,512]{1,0:T(8,128)(2,1)S(1)}, bf16[1536,512]{1,0:T(8,128)(2,1)S(1)}, u32[]{:S(2)}, u32[]{:S(2)}) collective-permute-start(bf16[1536,512]{1,0:T(8,128)(2,1)S(1)} %pad_maximum_fusion.20), channel_id=1, source_target_pairs={{0,1},{1,0},{2,3},{3,2},{4,5},{5,4},{6,7},{7,6},{8,9},{9,8},{10,11... | collective-permute-start | bytes 4718600 | tf_op jit(solution)/shard_map/ppermute | solution.py:512
  416.2 17.4 %collective-permute-start.23 = (bf16[2,1024,512]{2,1,0:T(8,128)(2,1)S(1)}, bf16[2,1024,512]{2,1,0:T(8,128)(2,1)S(1)}, u32[]{:S(2)}, u32[]{:S(2)}) collective-permute-start(bf16[2,1024,512]{2,1,0:T(8,128)(2,1)S(1)} %pad_maximum_fusion.15), channel_id=1, source_target_pairs={{0,2},{2,0},{1,3},{3,1},{4,6},{6,4},{5,7},{7,5},{8,10},{10,8},{9,1... | collective-permute-start | bytes 6291464 | tf_op jit(solution)/shard_map/ppermute | solution.py:512
  446.1 48.7 %collective-permute-start.29 = (bf16[1024,512]{1,0:T(8,128)(2,1)}, bf16[1024,512]{1,0:T(8,128)(2,1)}, u32[]{:S(2)}, u32[]{:S(2)}) collective-permute-start(bf16[1024,512]{1,0:T(8,128)(2,1)} %fusion.89), channel_id=1, source_target_pairs={{0,1},{1,0},{2,3},{3,2},{4,5},{5,4},{6,7},{7,6},{8,9},{9,8},{10,11... | collective-permute-start | bytes 3145736 | tf_op jit(solution)/shard_map/ppermute | solution.py:512
  479.9 13.4 %collective-permute-start.32 = (bf16[512,512]{1,0:T(8,128)(2,1)S(1)}, bf16[512,512]{1,0:T(8,128)(2,1)S(1)}, u32[]{:S(2)}, u32[]{:S(2)}) collective-permute-start(bf16[512,512]{1,0:T(8,128)(2,1)S(1)} %pad_maximum_fusion.30), channel_id=1, source_target_pairs={{0,1},{1,0},{2,3},{3,2},{4,5},{5,4},{6,7},{7,6},{8,9},{9,8},{10,11... | collective-permute-start | bytes 1572872 | tf_op jit(solution)/shard_map/ppermute | solution.py:512
  482.4 12.5 %collective-permute-start.30 = (bf16[2,512,512]{2,1,0:T(8,128)(2,1)S(1)}, bf16[2,512,512]{2,1,0:T(8,128)(2,1)S(1)}, u32[]{:S(2)}, u32[]{:S(2)}) collective-permute-start(bf16[2,512,512]{2,1,0:T(8,128)(2,1)S(1)} %pad_maximum_fusion.29), channel_id=1, source_target_pairs={{0,2},{2,0},{1,3},{3,1},{4,6},{6,4},{5,7},{7,5},{8,10},{10,8},{9,1... | collective-permute-start | bytes 3145736 | tf_op jit(solution)/shard_map/ppermute | solution.py:512
  495.3 14.4 %collective-permute-start.31 = (bf16[512,512]{1,0:T(8,128)(2,1)S(1)}, bf16[512,512]{1,0:T(8,128)(2,1)S(1)}, u32[]{:S(2)}, u32[]{:S(2)}) collective-permute-start(bf16[512,512]{1,0:T(8,128)(2,1)S(1)} %fusion.188), channel_id=1, source_target_pairs={{0,1},{1,0},{2,3},{3,2},{4,5},{5,4},{6,7},{7,6},{8,9},{9,8},{10,11... | collective-permute-start | bytes 1572872 | tf_op jit(solution)/shard_map/ppermute | solution.py:512
  511.6 403.9 %all-gather.3.cloned.1.call-start = ((), (), s32[]{:S(2)}) async-start(), calls=%async_computation | async-start | bytes 8912896 | tf_op jit(solution)/shard_map/all_gather | solution.py:906
  700.8 22.9 %collective-permute-start.34 = (bf16[3,1536,512]{2,1,0:T(8,128)(2,1)}, bf16[3,1536,512]{2,1,0:T(8,128)(2,1)}, u32[]{:S(2)}, u32[]{:S(2)}) collective-permute-start(bf16[3,1536,512]{2,1,0:T(8,128)(2,1)} %pad_maximum_fusion.4), channel_id=1, source_target_pairs={{0,2},{2,0},{1,3},{3,1},{4,6},{6,4},{5,7},{7,5},{8,10},{10,8},{9,1... | collective-permute-start | bytes 14155784 | tf_op jit(solution)/shard_map/ppermute | solution.py:512
  739.0 5.3 collective-permute-start.35
  780.1 24.0 %collective-permute-start.36 = (f32[512,512]{1,0:T(8,128)S(1)}, f32[512,512]{1,0:T(8,128)S(1)}, u32[]{:S(2)}, u32[]{:S(2)}) collective-permute-start(f32[512,512]{1,0:T(8,128)S(1)} %dynamic-slice_bitcast_fusion.6), channel_id=1, source_target_pairs={{0,1},{1,0},{2,3},{3,2},{4,5},{5,4},{6,7},{7,6},{8,9},{9,8},{10,11... | collective-permute-start | bytes 3145736 | tf_op jit(solution)/shard_map/ppermute | solution.py:512
  (330 other events, 2099.3 us)
Sparse Core Ops, SparseCore 0:
  511.7 183.8 all-reduce.14
  863.9 51.5 all-gather.2
